TPU v7x, 32 devices: a whole 2x2x4 slice. The times are simulated.
32 devices in a mesh: fsdp: 2 (over x), ctx: 4 (over y, core), tp: 4 (over z).
Axes of the slice: x: 2, y: 2, z: 4, core: 2. Of those that a mesh axis runs over, the one named last changes fastest.
Arguments:
- tokens: bfloat16 [8, 1024, 1024], P(('fsdp', 'tp'), 'ctx'), may hold values from -6 to 6
- cotangent: bfloat16 [8, 1024, 1024], P(('fsdp', 'tp'), 'ctx'), may hold values from -6 to 6
- mixer_gain: bfloat16 [1024], P(('fsdp', 'ctx', 'tp')), may hold values from 0.5 to 1.5
- mixer_input_weight: bfloat16 [1024, 3328], P(('fsdp', 'ctx', 'tp')), may hold values from -0.1875 to 0.1875
- step_weight: bfloat16 [1024, 24], P(('fsdp', 'ctx', 'tp')), may hold values from -0.1875 to 0.1875
- query_key_value_weight: bfloat16 [1024, 768], P(('fsdp', 'ctx', 'tp')), may hold values from -0.1875 to 0.1875
- conv_weight: bfloat16 [1792, 4], replicated, may hold values from -0.5 to 0.5
- conv_bias: bfloat16 [1792], replicated, may hold values from -0.5 to 0.5
- a_log: bfloat16 [24], replicated, may hold values from 0 to 2.765625
- step_bias: bfloat16 [24], replicated, may hold values from -6.875 to -2.296875
- skip_gain: bfloat16 [24], replicated, may hold values from 0.5 to 1.5
- mixer_output_weight: bfloat16 [1536, 1024], P(('fsdp', 'ctx', 'tp')), may hold values from -0.15625 to 0.15625
- attention_output_weight: bfloat16 [512, 1024], P(('fsdp', 'ctx', 'tp')), may hold values from -4 to 4
- mlp_gain: bfloat16 [1024], P(('fsdp', 'ctx', 'tp')), may hold values from 0.5 to 1.5
- gate_up_weight: bfloat16 [1024, 2, 2048], P(('fsdp', 'ctx'), None, 'tp'), may hold values from -0.1875 to 0.1875
- down_weight: bfloat16 [1024, 2048], P(('fsdp', 'ctx'), 'tp'), may hold values from -0.125 to 0.125
Outputs:
- out_block: bfloat16 [8, 1024, 1024], P(('fsdp', 'tp'), 'ctx')
- grad_tokens: bfloat16 [8, 1024, 1024], P(('fsdp', 'tp'), 'ctx')
- grad_mixer_gain: float32 [1024], P(('fsdp', 'ctx', 'tp'))
- grad_w_zx: float32 [1024, 3328], P(('fsdp', 'ctx', 'tp'))
- grad_w_step: float32 [1024, 24], P(('fsdp', 'ctx', 'tp'))
- grad_w_qkv: float32 [1024, 768], P(('fsdp', 'ctx', 'tp'))
- grad_conv_weight: float32 [1792, 4], replicated
- grad_conv_bias: float32 [1792], replicated
- grad_a_log: float32 [24], replicated
- grad_step_bias: float32 [24], replicated
- grad_skip_gain: float32 [24], replicated
- grad_w_mamba_out: float32 [1536, 1024], P(('fsdp', 'ctx', 'tp'))
- grad_w_attn_out: float32 [512, 1024], P(('fsdp', 'ctx', 'tp'))
- grad_mlp_gain: float32 [1024], P(('fsdp', 'ctx', 'tp'))
- grad_w_gate_up: float32 [1024, 2, 2048], P(('fsdp', 'ctx'), None, 'tp')
- grad_w_down: float32 [1024, 2048], P(('fsdp', 'ctx'), 'tp')
All inputs are finite; a program needn't handle non-finite values.
Results may differ from a plain program's by a relative error of at most 0.015.
The roundings to bfloat16 on the way count: a program that leaves them out, or rounds other values in their place, can miss the bound.
Values may be sent and summed in bfloat16 or wider, within the bound.
A program may use at most 192 MiB of HBM per device.

v0:
```python
import jax
import jax.numpy as jnp
from jax import lax
from jax.sharding import PartitionSpec as P

MH = 24
HD = 64
NS = 128
QH = 8
KVH = 2
SSD_BLK = 128
ATT_BLK = 512


def product(form, left, right):
    return jnp.einsum(form, left, right, preferred_element_type=jnp.float32)


def matrix_product(form, left, right):
    return jnp.einsum(form, left, right, precision=lax.Precision.HIGHEST)


def rms_scale(values_in):
    return lax.rsqrt(jnp.mean(values_in * values_in, axis=-1, keepdims=True) + 1e-05)


def norm_back(values_in, scale_in, gain_in, grad_normed):
    weighted = grad_normed * gain_in
    grad_values = scale_in * weighted - values_in * scale_in**3 * jnp.mean(
        weighted * values_in, axis=-1, keepdims=True
    )
    grad_gain = jnp.sum(grad_normed * values_in * scale_in, axis=(0, 1))
    return (grad_values, grad_gain)


def rotate(vectors, positions, direction):
    half_dim = HD // 2
    frequency = 10000.0 ** (-(jnp.arange(half_dim, dtype=jnp.float32) * 2.0 / HD))
    angles = positions.astype(jnp.float32)[:, None] * frequency[None, :]
    cosine = jnp.cos(angles)[:, None, :]
    sine_part = direction * jnp.sin(angles)[:, None, :]
    first_half = vectors[..., :half_dim]
    second = vectors[..., half_dim:]
    return jnp.concatenate(
        [first_half * cosine - second * sine_part, second * cosine + first_half * sine_part],
        axis=-1,
    )


def state_scan(
    input_values, input_matrix_projection, output_matrix_projection, step_length, rate_neg
):
    length, head_count, _ = input_values.shape
    blocks = length // SSD_BLK
    logarithmic_decay = step_length * rate_neg[None, :]
    triangle = jnp.arange(SSD_BLK)[:, None] >= jnp.arange(SSD_BLK)[None, :]

    def regroup_blocks(input_array):
        return input_array.reshape((blocks, SSD_BLK) + input_array.shape[1:])

    def state_move_forward(states, block_in):
        x_blk, b_blk, c_blk, step_blk, log_blk = block_in
        cumulative = jnp.cumsum(log_blk, axis=0)
        inner_cb = matrix_product("tn,sn->ts", c_blk, b_blk)
        spread = cumulative[:, None, :] - cumulative[None, :, :]
        mixing = (
            inner_cb[:, :, None]
            * jnp.exp(jnp.where(triangle[:, :, None], spread, -jnp.inf))
            * step_blk[None, :, :]
        )
        inside = matrix_product("tsh,shp->thp", mixing, x_blk)
        carried = matrix_product("tn,hpn->thp", c_blk, states) * jnp.exp(cumulative)[:, :, None]
        last_sum = cumulative[-1]
        fading = jnp.exp(last_sum[None, :] - cumulative) * step_blk
        renewed = jnp.exp(last_sum)[:, None, None] * states + matrix_product(
            "shp,sn->hpn", fading[:, :, None] * x_blk, b_blk
        )
        return (renewed, inside + carried)

    initial_state = jnp.zeros((head_count, HD, NS), jnp.float32)
    final_state, output_values = lax.scan(
        state_move_forward,
        initial_state,
        (
            regroup_blocks(input_values),
            regroup_blocks(input_matrix_projection),
            regroup_blocks(output_matrix_projection),
            regroup_blocks(step_length),
            regroup_blocks(logarithmic_decay),
        ),
    )
    return output_values.reshape(length, head_count, HD)


def mamba_seq(pre_conv, step_raw, conv_w, conv_b, log_rate, step_shift, skip_scale):
    length = pre_conv.shape[0]
    taps = conv_w.shape[1]
    padded = jnp.pad(pre_conv, ((taps - 1, 0), (0, 0)))
    conv_sum = jnp.broadcast_to(conv_b[None, :], pre_conv.shape)
    for offset in range(taps):
        conv_sum = conv_sum + padded[offset : offset + length] * conv_w[None, :, offset]
    activated = jax.nn.silu(conv_sum)
    head_count = step_raw.shape[1]
    input_values = activated[:, : head_count * HD].reshape(length, head_count, HD)
    input_matrix_projection = activated[:, head_count * HD : head_count * HD + NS]
    output_matrix_projection = activated[:, head_count * HD + NS :]
    step_length = jax.nn.softplus(step_raw + step_shift[None, :])
    output_values = state_scan(
        input_values,
        input_matrix_projection,
        output_matrix_projection,
        step_length,
        -jnp.exp(log_rate),
    )
    return (output_values + skip_scale[None, :, None] * input_values).reshape(
        length, head_count * HD
    )


def mamba_batch(pre_conv, step_raw, conv_w, conv_b, log_rate, step_shift, skip_scale):

    def mamba_one_seq(operands):
        return mamba_seq(operands[0], operands[1], conv_w, conv_b, log_rate, step_shift, skip_scale)

    return lax.map(jax.checkpoint(mamba_one_seq), (pre_conv, step_raw))


def masked_scores(query_blk, key_seq, row_start, key_pos):
    scores = product("qhd,khd->hqk", query_blk, key_seq) * HD ** (-0.5)
    query_pos = row_start + jnp.arange(ATT_BLK)
    return jnp.where(key_pos[None, None, :] <= query_pos[None, :, None], scores, -jnp.inf)


def attend_forward(queries, key_rot, values):
    seq_count, length, head_count, _ = queries.shape
    blocks = length // ATT_BLK
    key_pos = jnp.arange(length)

    def one_block(flat_index):
        seq_index = flat_index // blocks
        row_start = flat_index % blocks * ATT_BLK
        query_blk = lax.dynamic_slice(
            queries, (seq_index, row_start, 0, 0), (1, ATT_BLK, head_count, HD)
        )[0]
        key_seq = lax.dynamic_index_in_dim(key_rot, seq_index, 0, keepdims=False)
        value_seq = lax.dynamic_index_in_dim(values, seq_index, 0, keepdims=False)
        scores = masked_scores(query_blk, key_seq, row_start, key_pos)
        row_peak = jnp.max(scores, axis=-1, keepdims=True)
        raised = jnp.exp(scores - row_peak)
        totals = jnp.sum(raised, axis=-1, keepdims=True)
        attn_probs = raised / totals
        output = product("hqk,khd->qhd", attn_probs.astype(jnp.bfloat16), value_seq)
        return (output, row_peak[..., 0] + jnp.log(totals[..., 0]))

    output_values, logsum = lax.map(one_block, jnp.arange(seq_count * blocks))
    return (
        output_values.reshape(seq_count, length, head_count, HD),
        logsum.reshape(seq_count, blocks, head_count, ATT_BLK),
    )


def attend_backward(queries, key_rot, values, logsum, grad_out):
    seq_count, length, head_count, _ = queries.shape
    blocks = length // ATT_BLK
    key_pos = jnp.arange(length)
    score_scale = HD ** (-0.5)

    def attend_one_seq(operands):
        query_seq, key_seq, value_seq, logsum_seq, grad_seq = operands

        def one_move_forward(running, blk_index):
            grad_keys_acc, grad_values_acc = running
            row_start = blk_index * ATT_BLK
            query_blk = lax.dynamic_slice_in_dim(query_seq, row_start, ATT_BLK, 0)
            grad_blk = lax.dynamic_slice_in_dim(grad_seq, row_start, ATT_BLK, 0)
            scores = masked_scores(query_blk, key_seq, row_start, key_pos)
            attn_probs = jnp.exp(
                scores
                - lax.dynamic_index_in_dim(logsum_seq, blk_index, 0, keepdims=False)[:, :, None]
            )
            probs_low = attn_probs.astype(jnp.bfloat16)
            grad_probs = product("qhd,khd->hqk", grad_blk, value_seq)
            offset_mean = jnp.sum(attn_probs * grad_probs, axis=-1, keepdims=True)
            grad_scores = (attn_probs * (grad_probs - offset_mean)).astype(jnp.bfloat16)
            grad_query_blk = product("hqk,khd->qhd", grad_scores, key_seq) * score_scale
            grad_keys_acc = (
                grad_keys_acc + product("hqk,qhd->khd", grad_scores, query_blk) * score_scale
            )
            grad_values_acc = grad_values_acc + product("hqk,qhd->khd", probs_low, grad_blk)
            return ((grad_keys_acc, grad_values_acc), grad_query_blk)

        zeros_kv = jnp.zeros((length, head_count, HD), jnp.float32)
        (grad_keys_seq, grad_values_seq), grad_query_blocks = lax.scan(
            one_move_forward, (zeros_kv, zeros_kv), jnp.arange(blocks)
        )
        return (grad_query_blocks.reshape(length, head_count, HD), grad_keys_seq, grad_values_seq)

    return lax.map(attend_one_seq, (queries, key_rot, values, logsum, grad_out))


def on_device(
    tokens,
    cotangent,
    mixer_gain,
    mixer_input_weight,
    step_weight,
    query_key_value_weight,
    conv_weight,
    conv_bias,
    a_log,
    step_bias,
    skip_gain,
    mixer_output_weight,
    attention_output_weight,
    mlp_gain,
    gate_up_weight,
    down_weight,
):
    seq_count, local_len, _ = tokens.shape
    ctx_size = lax.axis_size("ctx")
    ctx_index = lax.axis_index("ctx")
    mamba_width = MH * HD
    heads_dev = MH // ctx_size
    query_dev = QH // ctx_size
    x_dev = heads_dev * HD
    q_dev = query_dev * HD
    full_len = local_len * ctx_size

    def gather_mixer():
        return (
            lax.all_gather(mixer_gain, ("fsdp", "ctx", "tp"), axis=0, tiled=True),
            lax.all_gather(mixer_input_weight, ("fsdp", "ctx", "tp"), axis=0, tiled=True),
            lax.all_gather(step_weight, ("fsdp", "ctx", "tp"), axis=0, tiled=True),
            lax.all_gather(query_key_value_weight, ("fsdp", "ctx", "tp"), axis=0, tiled=True),
            lax.all_gather(mixer_output_weight, ("fsdp", "ctx", "tp"), axis=0, tiled=True),
            lax.all_gather(attention_output_weight, ("fsdp", "ctx", "tp"), axis=0, tiled=True),
            lax.all_gather(mlp_gain, ("fsdp", "ctx", "tp"), axis=0, tiled=True),
        )

    def gather_mlp():
        return (
            lax.all_gather(gate_up_weight, ("fsdp", "ctx"), axis=0, tiled=True),
            lax.all_gather(down_weight, ("fsdp", "ctx"), axis=0, tiled=True),
        )

    gain_one, zx_full, step_full, qkv_full, mamba_proj, attn_proj, gain_two = gather_mixer()
    gate_up_full, down_full = gather_mlp()
    tokens_f = tokens.astype(jnp.float32)
    scale_one = rms_scale(tokens_f)
    first_normalized = (tokens_f * scale_one * gain_one.astype(jnp.float32)).astype(jnp.bfloat16)
    mixer_input_projection = product("gld,de->gle", first_normalized, zx_full)
    step_projection = product("gld,de->gle", first_normalized, step_full).astype(jnp.bfloat16)
    query_key_value_projection = product("gld,de->gle", first_normalized, qkv_full).astype(
        jnp.bfloat16
    )
    gate_z = mixer_input_projection[..., :mamba_width]
    conv_in = mixer_input_projection[..., mamba_width:].astype(jnp.bfloat16)
    x_pieces = conv_in[..., :mamba_width].reshape(seq_count, local_len, ctx_size, x_dev)
    bc_pieces = jnp.broadcast_to(
        conv_in[:, :, None, mamba_width:], (seq_count, local_len, ctx_size, 2 * NS)
    )
    query_pieces = query_key_value_projection[..., : QH * HD].reshape(
        seq_count, local_len, ctx_size, q_dev
    )
    key_heads = query_key_value_projection[..., QH * HD : (QH + KVH) * HD].reshape(
        seq_count, local_len, KVH, HD
    )
    value_heads = query_key_value_projection[..., (QH + KVH) * HD :].reshape(
        seq_count, local_len, KVH, HD
    )
    key_pieces = jnp.repeat(key_heads, QH // KVH, axis=2).reshape(
        seq_count, local_len, ctx_size, q_dev
    )
    value_pieces = jnp.repeat(value_heads, QH // KVH, axis=2).reshape(
        seq_count, local_len, ctx_size, q_dev
    )
    main_send = jnp.concatenate([x_pieces, query_pieces], axis=-1)
    shared_send = jnp.concatenate([bc_pieces, key_pieces, value_pieces], axis=-1)
    step_send = step_projection.reshape(seq_count, local_len, ctx_size, heads_dev)
    main_heads, shared_heads, step_heads = (
        lax.all_to_all(main_send, "ctx", split_axis=2, concat_axis=1, tiled=True),
        lax.all_to_all(shared_send, "ctx", split_axis=2, concat_axis=1, tiled=True),
        lax.all_to_all(step_send, "ctx", split_axis=2, concat_axis=1, tiled=True),
    )
    main_heads = main_heads[:, :, 0]
    shared_heads = shared_heads[:, :, 0]
    step_heads = step_heads[:, :, 0]
    key_width = (shared_heads.shape[-1] - 2 * NS) // 2
    kv_heads = key_width // HD
    conv_rows = jnp.concatenate(
        [
            lax.dynamic_slice_in_dim(conv_weight, ctx_index * x_dev, x_dev, 0),
            conv_weight[mamba_width:],
        ],
        axis=0,
    ).astype(jnp.float32)
    bias_rows = jnp.concatenate(
        [lax.dynamic_slice_in_dim(conv_bias, ctx_index * x_dev, x_dev, 0), conv_bias[mamba_width:]],
        axis=0,
    ).astype(jnp.float32)
    rate_rows = lax.dynamic_slice_in_dim(a_log, ctx_index * heads_dev, heads_dev, 0).astype(
        jnp.float32
    )
    shift_rows = lax.dynamic_slice_in_dim(step_bias, ctx_index * heads_dev, heads_dev, 0).astype(
        jnp.float32
    )
    skip_rows = lax.dynamic_slice_in_dim(skip_gain, ctx_index * heads_dev, heads_dev, 0).astype(
        jnp.float32
    )
    mamba_in = jnp.concatenate(
        [main_heads[..., :x_dev], shared_heads[..., : 2 * NS]], axis=-1
    ).astype(jnp.float32)
    mamba_out, mamba_pull = jax.vjp(
        mamba_batch,
        mamba_in,
        step_heads.astype(jnp.float32),
        conv_rows,
        bias_rows,
        rate_rows,
        shift_rows,
        skip_rows,
    )
    positions = jnp.arange(full_len)
    queries = rotate(
        main_heads[..., x_dev:].astype(jnp.float32).reshape(seq_count, full_len, query_dev, HD),
        positions,
        1.0,
    ).astype(jnp.bfloat16)
    key_rot = rotate(
        shared_heads[..., 2 * NS : 2 * NS + key_width]
        .astype(jnp.float32)
        .reshape(seq_count, full_len, kv_heads, HD),
        positions,
        1.0,
    ).astype(jnp.bfloat16)
    values = shared_heads[..., 2 * NS + key_width :].reshape(seq_count, full_len, kv_heads, HD)
    attn_out, logsum = attend_forward(queries, key_rot, values)
    back_send = jnp.concatenate(
        [
            mamba_out.astype(jnp.bfloat16),
            attn_out.reshape(seq_count, full_len, q_dev).astype(jnp.bfloat16),
        ],
        axis=-1,
    )[:, :, None, :]
    back_tokens = lax.all_to_all(back_send, "ctx", split_axis=1, concat_axis=2, tiled=True)
    mamba_tok = back_tokens[..., :x_dev].reshape(seq_count, local_len, mamba_width)
    attn_tok = back_tokens[..., x_dev:].reshape(seq_count, local_len, QH * HD)
    sig_z = jax.nn.sigmoid(gate_z)
    silu_z = gate_z * sig_z
    gated_mixture = (mamba_tok.astype(jnp.float32) * silu_z).astype(jnp.bfloat16)
    branch_output = product("gle,ed->gld", gated_mixture, mamba_proj) + product(
        "gle,ed->gld", attn_tok, attn_proj
    )
    residual_stream = tokens_f + branch_output
    scale_two = rms_scale(residual_stream)
    second_normalized = (residual_stream * scale_two * gain_two.astype(jnp.float32)).astype(
        jnp.bfloat16
    )
    rows_all = lax.all_gather(second_normalized, "tp", axis=0, tiled=True)
    gate_up_values = product("gld,dcf->glcf", rows_all, gate_up_full)
    gate_part = gate_up_values[..., 0, :]
    up_part = gate_up_values[..., 1, :]
    sig_gate = jax.nn.sigmoid(gate_part)
    silu_gate = gate_part * sig_gate
    hidden_units = (silu_gate * up_part).astype(jnp.bfloat16)
    partial_out = product("glf,df->gld", hidden_units, down_full)
    mlp_out = lax.psum_scatter(
        partial_out.astype(jnp.bfloat16), "tp", scatter_dimension=0, tiled=True
    ).astype(jnp.float32)
    out_block = (residual_stream + mlp_out).astype(jnp.bfloat16)
    gain_one, zx_full, step_full, qkv_full, mamba_proj, attn_proj, gain_two = gather_mixer()
    gate_up_full, down_full = gather_mlp()
    cot_all = lax.all_gather(cotangent, "tp", axis=0, tiled=True)
    grad_hidden = product("gld,df->glf", cot_all, down_full)
    grad_down = product("gld,glf->df", cot_all, hidden_units)
    slope_gate = sig_gate * (1.0 + gate_part * (1.0 - sig_gate))
    grad_gate_up = jnp.stack(
        [grad_hidden * up_part * slope_gate, grad_hidden * silu_gate], axis=2
    ).astype(jnp.bfloat16)
    grad_gu_w = product("gld,glcf->dcf", rows_all, grad_gate_up)
    grad_rows_part = product("glcf,dcf->gld", grad_gate_up, gate_up_full)
    grad_normed_two = lax.psum_scatter(
        grad_rows_part.astype(jnp.bfloat16), "tp", scatter_dimension=0, tiled=True
    ).astype(jnp.float32)
    grad_residual, grad_gain_two = norm_back(
        residual_stream, scale_two, gain_two.astype(jnp.float32), grad_normed_two
    )
    grad_residual = grad_residual + cotangent.astype(jnp.float32)
    grad_branch = grad_residual.astype(jnp.bfloat16)
    grad_mamba_proj = product("gle,gld->ed", gated_mixture, grad_branch)
    grad_attn_proj = product("gle,gld->ed", attn_tok, grad_branch)
    grad_gated = product("gld,ed->gle", grad_branch, mamba_proj)
    slope_z = sig_z * (1.0 + gate_z * (1.0 - sig_z))
    grad_mamba_tok = (grad_gated * silu_z).astype(jnp.bfloat16)
    grad_z = grad_gated * mamba_tok.astype(jnp.float32) * slope_z
    grad_attn_tok = product("gld,ed->gle", grad_branch, attn_proj).astype(jnp.bfloat16)
    grad_send = jnp.concatenate(
        [
            grad_mamba_tok.reshape(seq_count, local_len, ctx_size, x_dev),
            grad_attn_tok.reshape(seq_count, local_len, ctx_size, q_dev),
        ],
        axis=-1,
    )
    grad_heads = lax.all_to_all(grad_send, "ctx", split_axis=2, concat_axis=1, tiled=True)[:, :, 0]
    grad_pre, grad_step, grad_conv_w, grad_conv_b, grad_rate, grad_shift, grad_skip = mamba_pull(
        grad_heads[..., :x_dev].astype(jnp.float32)
    )
    grad_queries, grad_keys, grad_values = attend_backward(
        queries,
        key_rot,
        values,
        logsum,
        grad_heads[..., x_dev:].reshape(seq_count, full_len, query_dev, HD),
    )
    grad_queries = rotate(grad_queries, positions, -1.0)
    grad_keys = rotate(grad_keys, positions, -1.0)
    main_back = jnp.concatenate(
        [grad_pre[..., :x_dev], grad_queries.reshape(seq_count, full_len, q_dev)], axis=-1
    )[:, :, None, :]
    shared_back = jnp.concatenate(
        [
            grad_pre[..., x_dev:],
            grad_keys.reshape(seq_count, full_len, key_width),
            grad_values.reshape(seq_count, full_len, key_width),
        ],
        axis=-1,
    )[:, :, None, :]
    main_tok, shared_tok, step_tok = (
        lax.all_to_all(
            main_back.astype(jnp.bfloat16), "ctx", split_axis=1, concat_axis=2, tiled=True
        ).astype(main_back.dtype),
        lax.all_to_all(
            shared_back.astype(jnp.bfloat16), "ctx", split_axis=1, concat_axis=2, tiled=True
        ).astype(shared_back.dtype),
        lax.all_to_all(
            grad_step[:, :, None, :].astype(jnp.bfloat16),
            "ctx",
            split_axis=1,
            concat_axis=2,
            tiled=True,
        ).astype(jnp.float32),
    )
    grad_x_conv = main_tok[..., :x_dev].reshape(seq_count, local_len, mamba_width)
    grad_query_tok = main_tok[..., x_dev:].reshape(seq_count, local_len, QH * HD)
    grad_bc = jnp.sum(shared_tok[..., : 2 * NS], axis=2)
    grad_key_tok = jnp.sum(
        shared_tok[..., 2 * NS : 2 * NS + key_width].reshape(seq_count, local_len, KVH, -1, HD),
        axis=3,
    ).reshape(seq_count, local_len, KVH * HD)
    grad_value_tok = jnp.sum(
        shared_tok[..., 2 * NS + key_width :].reshape(seq_count, local_len, KVH, -1, HD), axis=3
    ).reshape(seq_count, local_len, KVH * HD)
    grad_zx = jnp.concatenate([grad_z, grad_x_conv, grad_bc], axis=-1).astype(jnp.bfloat16)
    grad_step_low = step_tok.reshape(seq_count, local_len, MH).astype(jnp.bfloat16)
    grad_qkv = jnp.concatenate([grad_query_tok, grad_key_tok, grad_value_tok], axis=-1).astype(
        jnp.bfloat16
    )
    grad_normed_one = (
        product("gle,de->gld", grad_zx, zx_full)
        + product("gle,de->gld", grad_step_low, step_full)
        + product("gle,de->gld", grad_qkv, qkv_full)
    )
    grad_zx_w = product("gld,gle->de", first_normalized, grad_zx)
    grad_step_w = product("gld,gle->de", first_normalized, grad_step_low)
    grad_qkv_w = product("gld,gle->de", first_normalized, grad_qkv)
    grad_input, grad_gain_one = norm_back(
        tokens_f, scale_one, gain_one.astype(jnp.float32), grad_normed_one
    )
    grad_input = grad_input + grad_residual
    mixer_sums = (
        lax.psum_scatter(grad_gain_one, ("fsdp", "ctx", "tp"), scatter_dimension=0, tiled=True),
        lax.psum_scatter(grad_zx_w, ("fsdp", "ctx", "tp"), scatter_dimension=0, tiled=True),
        lax.psum_scatter(grad_step_w, ("fsdp", "ctx", "tp"), scatter_dimension=0, tiled=True),
        lax.psum_scatter(grad_qkv_w, ("fsdp", "ctx", "tp"), scatter_dimension=0, tiled=True),
        lax.psum_scatter(grad_mamba_proj, ("fsdp", "ctx", "tp"), scatter_dimension=0, tiled=True),
        lax.psum_scatter(grad_attn_proj, ("fsdp", "ctx", "tp"), scatter_dimension=0, tiled=True),
        lax.psum_scatter(grad_gain_two, ("fsdp", "ctx", "tp"), scatter_dimension=0, tiled=True),
    )
    mlp_sums = (
        lax.psum_scatter(grad_gu_w, ("fsdp", "ctx"), scatter_dimension=0, tiled=True),
        lax.psum_scatter(grad_down, ("fsdp", "ctx"), scatter_dimension=0, tiled=True),
    )
    conv_full = jnp.concatenate(
        [
            lax.dynamic_update_slice_in_dim(
                jnp.zeros((mamba_width, grad_conv_w.shape[1]), jnp.float32),
                grad_conv_w[:x_dev],
                ctx_index * x_dev,
                0,
            ),
            grad_conv_w[x_dev:],
        ],
        axis=0,
    )
    bias_full = jnp.concatenate(
        [
            lax.dynamic_update_slice_in_dim(
                jnp.zeros((mamba_width,), jnp.float32), grad_conv_b[:x_dev], ctx_index * x_dev, 0
            ),
            grad_conv_b[x_dev:],
        ],
        axis=0,
    )
    rate_full = lax.dynamic_update_slice_in_dim(
        jnp.zeros((MH,), jnp.float32), grad_rate, ctx_index * heads_dev, 0
    )
    shift_full = lax.dynamic_update_slice_in_dim(
        jnp.zeros((MH,), jnp.float32), grad_shift, ctx_index * heads_dev, 0
    )
    skip_full = lax.dynamic_update_slice_in_dim(
        jnp.zeros((MH,), jnp.float32), grad_skip, ctx_index * heads_dev, 0
    )
    head_sums = lax.psum(
        (conv_full, bias_full, rate_full, shift_full, skip_full), ("fsdp", "ctx", "tp")
    )
    return (
        out_block,
        grad_input.astype(jnp.bfloat16),
        mixer_sums[0],
        mixer_sums[1],
        mixer_sums[2],
        mixer_sums[3],
        head_sums[0],
        head_sums[1],
        head_sums[2],
        head_sums[3],
        head_sums[4],
        mixer_sums[4],
        mixer_sums[5],
        mixer_sums[6],
        mlp_sums[0],
        mlp_sums[1],
    )


def solution(mesh):
    placed = (
        P(("fsdp", "tp"), "ctx", None),
        P(("fsdp", "tp"), "ctx", None),
        P(("fsdp", "ctx", "tp")),
        P(("fsdp", "ctx", "tp"), None),
        P(("fsdp", "ctx", "tp"), None),
        P(("fsdp", "ctx", "tp"), None),
        P(),
        P(),
        P(),
        P(),
        P(),
        P(("fsdp", "ctx", "tp"), None),
        P(("fsdp", "ctx", "tp"), None),
        P(("fsdp", "ctx", "tp")),
        P(("fsdp", "ctx"), None, "tp"),
        P(("fsdp", "ctx"), "tp"),
    )
    return jax.shard_map(
        on_device,
        mesh=mesh,
        in_specs=placed,
        out_specs=(
            P(("fsdp", "tp"), "ctx", None),
            P(("fsdp", "tp"), "ctx", None),
            P(("fsdp", "ctx", "tp")),
            P(("fsdp", "ctx", "tp"), None),
            P(("fsdp", "ctx", "tp"), None),
            P(("fsdp", "ctx", "tp"), None),
            P(),
            P(),
            P(),
            P(),
            P(),
            P(("fsdp", "ctx", "tp"), None),
            P(("fsdp", "ctx", "tp"), None),
            P(("fsdp", "ctx", "tp")),
            P(("fsdp", "ctx"), None, "tp"),
            P(("fsdp", "ctx"), "tp"),
        ),
        check_vma=False,
    )
```

profile of v0, /device:TPU:0, one launch (start us, length us, event | category | flops | bytes accessed | tf_op | source)
XLA Modules:
  0.0 1993.6 jit_solution(5119949987613282481)
XLA Ops:
  11.8 42.1 %all-reduce.19 = (bf16[1024]{0:T(1024)(128)(2,1)S(1)}, bf16[1024]{0:T(1024)(128)(2,1)}) all-reduce(bf16[1024]{0:T(1024)(128)(2,1)S(1)} %dynamic-update-slice, bf16[1024]{0:T(1024)(128)(2,1)S(1)} %dynamic-update-slice.1), channel_id=1, replica_groups=mesh['fsdp'=2,'ctx'=4,'tp'=4] {'fsdp','ctx','tp'}, use_global_device_ids=true, to_apply=%add.14 | all-reduce | flops 2048 | bytes 8192
  53.9 68.7 %all-gather = bf16[32,32,24]{1,2,0:T(8,128)(2,1)S(1)} all-gather(bf16[1,32,24]{1,2,0:T(8,128)(2,1)} %bitcast.837), channel_id=1, replica_groups=mesh['fsdp'=2,'ctx'=4,'tp'=4] {'fsdp','ctx','tp'}, dimensions={0}, use_global_device_ids=true | all-gather | bytes 50688 | tf_op jit(solution)/shard_map/all_gather | solution.py:233
  142.5 6.7 fusion.257
  159.0 9.8 all-to-all-done.2
  175.7 11.3 all-to-all-done.1
  205.5 158.9 %while.161 = (s32[]{:T(128)}, f32[6,64,128]{2,1,0:T(8,128)S(1)}, f32[8,128,6,64]{1,0,3,2:T(8,128)}, f32[8,128,6]{1,0,2:T(8,128)}, f32[8,128,6]{1,0,2:T(8,128)}, ...) while((s32[]{:T(128)}, f32[6,64,128]{2,1,0:T(8,128)S(1)}, ...), condition=%wide.region_3.4_spmd.clone, body=%wide.region_1.3_spmd.clone.sunk | while | flops 252494592 | bytes 2852632 | solution.py:81
  219.3 6.1 dynamic_update_slice.248
  239.1 6.1 dynamic_update_slice.248
  259.0 6.1 dynamic_update_slice.248
  278.9 6.1 dynamic_update_slice.248
  298.8 6.1 dynamic_update_slice.248
  318.6 6.1 dynamic_update_slice.248
  338.5 6.1 dynamic_update_slice.248
  358.3 6.1 dynamic_update_slice.248
  367.9 19.3 while.160
  403.4 9.0 reduce.27
  420.5 14.4 all-to-all-done.3
  459.8 43.3 %all-gather.18.cloned.1.call-done = bf16[4,256,1024]{2,1,0:T(8,128)(2,1)} async-done(((bf16[1,256,1024]{2,1,0:T(8,128)(2,1)}), bf16[4,256,1024]{2,1,0:T(8,128)(2,1)}) %all-gather.18.cloned.1.call-update) | async-done | bytes 2097168 | tf_op jit(solution)/shard_map/all_gather | solution.py:359
  503.1 6.6 fusion.180
  509.6 17.6 all-gather.22.cloned.1.call-done
  527.2 47.5 %all-gather.24.cloned.1.call-done = bf16[4,256,1024]{2,1,0:T(8,128)(2,1)} async-done(((bf16[1,256,1024]{2,1,0:T(8,128)(2,1)}), bf16[4,256,1024]{2,1,0:T(8,128)(2,1)}) %all-gather.24.cloned.1.call-update) | async-done | bytes 2097168 | tf_op jit(solution)/shard_map/all_gather | solution.py:373
  574.7 6.3 fusion.212
  589.8 39.1 %reduce-scatter.14.cloned.1.call-done = bf16[1,256,1024]{2,1,0:T(8,128)(2,1)} async-done(((bf16[4,256,1024]{2,1,0:T(8,128)(2,1)}), bf16[1,256,1024]{2,1,0:T(8,128)(2,1)}) %reduce-scatter.14.cloned.1.call-update) | async-done | bytes 524304 | tf_op jit(solution)/shard_map/reduce_scatter | solution.py:382
  652.6 9.6 all-to-all-done.4
  687.4 132.0 %while.162 = (s32[]{:T(128)}, f32[6,64,128]{2,1,0:T(8,128)S(1)}, f32[8,6]{1,0:T(8,128)}, f32[8,6,64,128]{3,2,1,0:T(8,128)}, f32[8,6,1,1]{1,3,2,0:T(1,128)}, /*in...) while((s32[]{:T(128)}, f32[6,64,128]{2,1,0:T(8,128)S(1)}, ...), condition=%wide.region_14.15_spmd.clone, body=%wide.region_12.14_spmd.clone.sunk | while | flops 176999424 | bytes 3585603 | solution.py:81
  823.8 250.6 %while.163 = (s32[]{:T(128)}, f32[6,64,128]{2,1,0:T(8,128)S(1)}, f32[8,128,6,64]{1,0,3,2:T(8,128)}, f32[8,128,128]{2,1,0:T(8,128)}, f32[8,128,128]{2,1,0:T(8,128...) while((s32[]{:T(128)}, f32[6,64,128]{2,1,0:T(8,128)S(1)}, ...), condition=%wide.region_25.26_spmd.clone, body=%wide.region_15.25_spmd.clone.sunk | while | flops 505206784 | bytes 6947109 | solution.py:81
  849.0 6.1 dynamic_update_slice.263
  880.4 6.1 dynamic_update_slice.263
  911.6 6.1 dynamic_update_slice.263
  943.0 6.1 dynamic_update_slice.263
  974.2 6.1 dynamic_update_slice.263
  1005.6 6.1 dynamic_update_slice.263
  1036.9 6.1 dynamic_update_slice.263
  1068.2 6.1 dynamic_update_slice.263
  1083.9 6.2 all_to_all.108
  1098.2 6.6 convolution_bitcast_fusion.7
  1112.6 45.7 %while.164 = (s32[]{:T(128)}, f32[1024,2,64]{0,2,1:T(8,128)}, f32[1024,2,64]{0,2,1:T(8,128)}, f32[2,512,2,64]{1,0,3,2:T(2,128)}, s32[2]{0:T(128)}, /*index=5*/bf...) while((s32[]{:T(128)}, f32[1024,2,64]{0,2,1:T(8,128)}, ...), condition=%wide.region_28.29_spmd.clone, body=%wide.region_26.28_spmd.clone.sunk | while | flops 688061952 | bytes 38306068 | solution.py:193
  1152.6 5.8 dynamic_update_slice.264
  1180.9 8.1 reduce.28
  1199.5 7.0 reduce.29
  1222.9 8.2 all-to-all-done.5
  1251.0 7.0 fusion.217
  1273.5 39.7 %all-reduce.18 = (f32[1024]{0:T(1024)S(1)}, f32[1792,4]{0,1:T(4,128)}, f32[1792]{0:T(1024)}, f32[24]{0:T(128)}, f32[24]{0:T(128)}, /*index=5*/f32[24]{0:T(128)}, f32[1024]{0:T(1024)S(1)}) all-reduce(f32[1024]{0:T(1024)S(1)} %get-tuple-element.1826, ...), channel_id=4, replica_groups=mesh['fsdp'=2,'ctx'=4,'tp'=4] {'fsdp','ctx','tp'}, use_global_device_ids=true, to_apply=%region_34.35.clone | all-reduce | flops 11080 | bytes 88640
  1317.6 6.4 reduce-scatter.24.cloned.1.call-done
  1326.3 138.7 %reduce-scatter.22.cloned.1.call-done = f32[16,1024]{1,0:T(8,128)} async-done(((f32[512,1024]{1,0:T(8,128)}), f32[16,1024]{1,0:T(8,128)}) %reduce-scatter.22.cloned.1.call-update) | async-done | bytes 65552 | tf_op jit(solution)/shard_map/reduce_scatter | solution.py:476
  1465.0 105.4 %reduce-scatter.18.cloned.1.call-done = f32[32,768]{1,0:T(8,128)} async-done(((f32[1024,768]{1,0:T(8,128)}), f32[32,768]{1,0:T(8,128)}) %reduce-scatter.18.cloned.1.call-update) | async-done | bytes 98320 | tf_op jit(solution)/shard_map/reduce_scatter | solution.py:474
  1570.4 119.6 %reduce-scatter.20.cloned.1.call-done = f32[48,1024]{1,0:T(8,128)} async-done(((f32[1536,1024]{1,0:T(8,128)}), f32[48,1024]{1,0:T(8,128)}) %reduce-scatter.20.cloned.1.call-update) | async-done | bytes 196624 | tf_op jit(solution)/shard_map/reduce_scatter | solution.py:475
  1690.0 296.9 %reduce-scatter.16.cloned.1.call-done = f32[32,3328]{1,0:T(8,128)} async-done(((f32[1024,3328]{1,0:T(8,128)}), f32[32,3328]{1,0:T(8,128)}) %reduce-scatter.16.cloned.1.call-update) | async-done | bytes 426000 | tf_op jit(solution)/shard_map/reduce_scatter | solution.py:472
  (1097 shorter events, 782.6 us)
Async XLA Ops:
  7.2 126.6 %copy-start.3 = (bf16[1,256,1024]{2,1,0:T(8,128)(2,1)S(1)}, bf16[1,256,1024]{2,1,0:T(8,128)(2,1)}, u32[]{:S(2)}) copy-start(bf16[1,256,1024]{2,1,0:T(8,128)(2,1)} %param.26) | copy-start | bytes 1572868
  7.2 122.8 %copy-start.46 = (bf16[128,2,512]{2,1,0:T(2,128)(2,1)S(1)}, bf16[128,2,512]{2,1,0:T(2,128)(2,1)}, u32[]{:S(2)}) copy-start(bf16[128,2,512]{2,1,0:T(2,128)(2,1)} %param.40) | copy-start | bytes 786436
  7.2 125.0 %copy-start.89 = (bf16[1792,4]{0,1:T(4,128)(2,1)S(1)}, bf16[1792,4]{0,1:T(4,128)(2,1)}, u32[]{:S(2)}) copy-start(bf16[1792,4]{0,1:T(4,128)(2,1)} %param.32) | copy-start | bytes 43012
  7.2 126.5 %slice-start = ((bf16[1792,4]{0,1:T(4,128)(2,1)}), bf16[256,4]{0,1:T(4,128)(2,1)S(1)}, s32[]{:S(2)}) async-start(bf16[1792,4]{0,1:T(4,128)(2,1)} %param.32), calls=%async_computation.34 | async-start | bytes 4096 | tf_op jit(solution)/shard_map/slice | solution.py:293
  7.2 125.1 %copy-start.104 = (bf16[24]{0:T(256)(128)(2,1)S(1)}, bf16[24]{0:T(256)(128)(2,1)}, u32[]{:S(2)}) copy-start(bf16[24]{0:T(256)(128)(2,1)} %param.34) | copy-start | bytes 148
  7.2 125.7 %copy-start.102 = (bf16[24]{0:T(256)(128)(2,1)S(1)}, bf16[24]{0:T(256)(128)(2,1)}, u32[]{:S(2)}) copy-start(bf16[24]{0:T(256)(128)(2,1)} %param.36) | copy-start | bytes 148
  7.2 125.7 %copy-start.103 = (bf16[24]{0:T(256)(128)(2,1)S(1)}, bf16[24]{0:T(256)(128)(2,1)}, u32[]{:S(2)}) copy-start(bf16[24]{0:T(256)(128)(2,1)} %param.35) | copy-start | bytes 148
  7.3 126.5 %all-gather.12.cloned.1.call-start = ((), (), s32[]{:S(2)}) async-start(), calls=%async_computation.18 | async-start | bytes 1622016 | tf_op jit(solution)/shard_map/all_gather | solution.py:234
  8.0 134.5 %all-gather.10.cloned.1.call-start = ((), (), s32[]{:S(2)}) async-start(), calls=%async_computation.17 | async-start | bytes 7028736 | tf_op jit(solution)/shard_map/all_gather | solution.py:232
  8.7 441.2 %all-gather.14.cloned.1.call-start = ((), (), s32[]{:S(2)}) async-start(), calls=%async_computation.19 | async-start | bytes 3244032 | tf_op jit(solution)/shard_map/all_gather | solution.py:235
  9.5 444.5 %all-gather.16.cloned.1.call-start = ((), (), s32[]{:S(2)}) async-start(), calls=%async_computation.20 | async-start | bytes 1081344 | tf_op jit(solution)/shard_map/all_gather | solution.py:236
  53.9 88.6 %copy-start.33 = (f32[1024]{0:T(1024)}, f32[1024]{0:T(1024)S(1)}, u32[]{:S(2)}) copy-start(f32[1024]{0:T(1024)S(1)} %convert_element_type.330) | copy-start | bytes 12292
  126.7 23.8 %all-to-all-start = ((bf16[1,256,4,6]{1,3,0,2:T(8,128)(2,1)}), bf16[1,256,4,6]{1,3,0,2:T(8,128)(2,1)S(1)}, u32[]{:S(2)}, u32[]{:S(2)}) async-start(bf16[1,256,4,6]{1,3,0,2:T(8,128)(2,1)} %bitcast.2), calls=%async_computation | async-start | bytes 32768 | tf_op jit(solution)/shard_map/all_to_all | solution.py:283
  130.0 329.8 %all-gather.20.cloned.1.call-start = ((), (), s32[]{:S(2)}) async-start(), calls=%async_computation.22 | async-start | bytes 2359296 | tf_op jit(solution)/shard_map/all_gather | solution.py:242
  133.0 40.2 %copy-start.86 = (f32[6]{0:T(128)}, f32[6]{0:T(128)S(1)}, u32[]{:S(2)}) copy-start(f32[6]{0:T(128)S(1)} %get-tuple-element.1112) | copy-start | bytes 76
  133.7 54.6 %copy-start.70 = (f32[640]{0:T(1024)}, f32[640]{0:T(1024)S(1)}, u32[]{:S(2)}) copy-start(f32[640]{0:T(1024)S(1)} %maximum_convert_fusion.2) | copy-start | bytes 7684
  133.8 20.6 %copy-start.52 = (f32[640,4]{0,1:T(4,128)}, f32[640,4]{0,1:T(4,128)S(1)}, u32[]{:S(2)}) copy-start(f32[640,4]{0,1:T(4,128)S(1)} %maximum_convert_fusion.1) | copy-start | bytes 30724
  150.8 18.0 all-to-all-start.2
  168.7 18.2 all-to-all-start.1
  416.2 18.8 all-to-all-start.3
  420.4 82.7 %all-gather.18.cloned.1.call-start = ((), (), s32[]{:S(2)}) async-start(), calls=%async_computation.21 | async-start | bytes 2621440 | tf_op jit(solution)/shard_map/all_gather | solution.py:359
  420.5 210.7 %copy-start.50 = (f32[1024]{0:T(1024)}, f32[1024]{0:T(1024)S(1)}, u32[]{:S(2)}) copy-start(f32[1024]{0:T(1024)S(1)} %convert_element_type.353) | copy-start | bytes 12292
  456.2 175.0 %copy-start.73 = (f32[256]{0:T(256)}, f32[256]{0:T(256)S(1)}, u32[]{:S(2)}) copy-start(f32[256]{0:T(256)S(1)} %get-tuple-element.2082) | copy-start | bytes 3076
  456.2 175.0 %copy-start.81 = (f32[256]{0:T(256)}, f32[256]{0:T(256)S(1)}, u32[]{:S(2)}) copy-start(f32[256]{0:T(256)S(1)} %get-tuple-element.2081) | copy-start | bytes 3076
  458.2 69.0 %all-gather.22.cloned.1.call-start = ((), (), s32[]{:S(2)}) async-start(), calls=%async_computation.23 | async-start | bytes 1179648 | tf_op jit(solution)/shard_map/all_gather | solution.py:243
  459.0 115.8 %all-gather.24.cloned.1.call-start = ((), (), s32[]{:S(2)}) async-start(), calls=%async_computation.25 | async-start | bytes 2621440 | tf_op jit(solution)/shard_map/all_gather | solution.py:373
  459.7 169.1 %reduce-scatter.14.cloned.1.call-start = ((), (), s32[]{:S(2)}) async-start(), calls=%async_computation.26 | async-start | bytes 2621440 | tf_op jit(solution)/shard_map/reduce_scatter | solution.py:382
  643.4 18.8 all-to-all-start.4
  647.7 610.4 %reduce-scatter.26.cloned.1.call-start = ((), (), s32[]{:S(2)}) async-start(), calls=%async_computation.32 | async-start | bytes 2359296 | tf_op jit(solution)/shard_map/reduce_scatter | solution.py:481
  652.6 612.0 %reduce-scatter.28.cloned.1.call-start = ((), (), s32[]{:S(2)}) async-start(), calls=%async_computation.33 | async-start | bytes 540672
  1093.9 220.5 %reduce-scatter.12.cloned.1.call-start = ((), (), s32[]{:S(2)}) async-start(), calls=%async_computation.24 | async-start | bytes 2621440 | tf_op jit(solution)/shard_map/reduce_scatter | solution.py:367
  1098.2 225.9 %reduce-scatter.24.cloned.1.call-start = ((), (), s32[]{:S(2)}) async-start(), calls=%async_computation.31 | async-start | bytes 4718592 | tf_op jit(solution)/shard_map/reduce_scatter | solution.py:480
  1104.8 360.2 %reduce-scatter.22.cloned.1.call-start = ((), (), s32[]{:S(2)}) async-start(), calls=%async_computation.30 | async-start | bytes 2162688 | tf_op jit(solution)/shard_map/reduce_scatter | solution.py:476
  1112.6 47.2 %copy-start.21 = (f32[1024,32]{0,1:T(8,128)S(1)}, f32[1024,32]{0,1:T(8,128)}, u32[]{:S(2)}) copy-start(f32[1024,32]{0,1:T(8,128)} %get-tuple-element.2078) | copy-start | bytes 393220
  1192.7 19.5 all-to-all-start.6
  1212.3 18.9 all-to-all-start.5
  1216.5 353.9 %reduce-scatter.18.cloned.1.call-start = ((), (), s32[]{:S(2)}) async-start(), calls=%async_computation.28 | async-start | bytes 3244032 | tf_op jit(solution)/shard_map/reduce_scatter | solution.py:474
  1243.7 446.3 %reduce-scatter.20.cloned.1.call-start = ((), (), s32[]{:S(2)}) async-start(), calls=%async_computation.29 | async-start | bytes 6488064 | tf_op jit(solution)/shard_map/reduce_scatter | solution.py:475
  1248.8 738.1 %reduce-scatter.16.cloned.1.call-start = ((), (), s32[]{:S(2)}) async-start(), calls=%async_computation.27 | async-start | bytes 14057472 | tf_op jit(solution)/shard_map/reduce_scatter | solution.py:472
  1271.6 42.9 %copy-start.1 = (f32[1,256,1024]{2,1,0:T(8,128)S(1)}, f32[1,256,1024]{2,1,0:T(8,128)}, u32[]{:S(2)}) copy-start(f32[1,256,1024]{2,1,0:T(8,128)} %copy-done) | copy-start | bytes 3145732
  1271.6 42.9 %copy-start.11 = (bf16[1,256,1024]{2,1,0:T(8,128)(2,1)S(1)}, bf16[1,256,1024]{2,1,0:T(8,128)(2,1)}, u32[]{:S(2)}) copy-start(bf16[1,256,1024]{2,1,0:T(8,128)(2,1)} %param.27) | copy-start | bytes 1572868
  1271.6 42.9 %copy-start.12 = (bf16[1,256,1024]{2,1,0:T(8,128)(2,1)S(1)}, bf16[1,256,1024]{2,1,0:T(8,128)(2,1)}, u32[]{:S(2)}) copy-start(bf16[1,256,1024]{2,1,0:T(8,128)(2,1)} %reduce-scatter.14.cloned.1.call-done) | copy-start | bytes 1572868
  1271.6 42.9 %copy-start.51 = (f32[1024]{0:T(1024)S(1)}, f32[1024]{0:T(1024)}, u32[]{:S(2)}) copy-start(f32[1024]{0:T(1024)} %copy-done.50) | copy-start | bytes 12292
  1271.6 42.9 %copy-start.59 = (f32[256]{0:T(256)S(1)}, f32[256]{0:T(256)}, u32[]{:S(2)}) copy-start(f32[256]{0:T(256)} %copy-done.54) | copy-start | bytes 3076
  1271.6 42.9 %copy-start.74 = (f32[256]{0:T(256)S(1)}, f32[256]{0:T(256)}, u32[]{:S(2)}) copy-start(f32[256]{0:T(256)} %copy-done.73) | copy-start | bytes 3076
  1271.6 42.9 %copy-start.82 = (f32[256]{0:T(256)S(1)}, f32[256]{0:T(256)}, u32[]{:S(2)}) copy-start(f32[256]{0:T(256)} %copy-done.81) | copy-start | bytes 3076
  1271.6 42.9 %copy-start.84 = (f32[256]{0:T(256)S(1)}, f32[256]{0:T(256)}, u32[]{:S(2)}) copy-start(f32[256]{0:T(256)} %copy-done.83) | copy-start | bytes 3076
  1271.6 42.9 %copy-start.91 = (f32[256]{0:T(256)S(1)}, f32[256]{0:T(256)}, u32[]{:S(2)}) copy-start(f32[256]{0:T(256)} %get-tuple-element.2079) | copy-start | bytes 3076
  (90 other events, 376.7 us)
Sparse Core Ops, SparseCore 0:
  11.0 57.8 all-gather.11
  71.7 70.7 all-gather.9
  145.4 57.7 all-gather.13
  206.0 52.5 all-gather.15
  260.4 26.9 all-gather.19
  458.3 44.6 all-gather.17
  504.9 22.1 all-gather.21
  528.8 45.9 all-gather.23
  586.2 42.5 reduce-scatter.13
  652.7 41.0 reduce-scatter.25
  1094.1 133.0 reduce-scatter.27
  1229.4 40.3 reduce-scatter.11
  1273.2 50.8 reduce-scatter.23
  1326.8 138.1 reduce-scatter.21
  1470.9 99.5 reduce-scatter.17
  1576.5 113.4 reduce-scatter.19
  1692.9 293.9 reduce-scatter.15
where the time goes:
time: 2010 us; the launch traced here: 1990 us
  waiting for transfers between devices  881 us (44%)
  local copies, waits for them, and re-layouts  410 us (20%)
  matrix products  295 us (15%)
  other arithmetic  195 us (10%)
  blocking collectives  157 us (8%)
  starting transfers between devices  29 us (1%)
    reduce_scatter x1, waiting for transfers between devices, on_device(): lax.psum_scatter(grad_zx_w, ('fsdp', 'ctx', 'tp'), scatter_dimension=0, t...  297 us
    dot_general x120, matrix products, matrix_product(): return jnp.einsum(form, left, right, precision=lax.Precision.HIGHEST)  186 us
    reduce_scatter x1, waiting for transfers between devices, on_device(): lax.psum_scatter(grad_attn_proj, ('fsdp', 'ctx', 'tp'), scatter_dimension...  139 us
    dynamic_update_slice x104, local copies, waits for them, and re-layouts, state_scan(): lax.scan(state_move_forward, initial_state, (regroup_blocks(input_values)...  135 us
    reduce_scatter x1, waiting for transfers between devices, on_device(): lax.psum_scatter(grad_mamba_proj, ('fsdp', 'ctx', 'tp'), scatter_dimensio...  120 us
    dot_general x34, matrix products, product(): return jnp.einsum(form, left, right, preferred_element_type=jnp.float32)  108 us
    reduce_scatter x1, waiting for transfers between devices, on_device(): lax.psum_scatter(grad_qkv_w, ('fsdp', 'ctx', 'tp'), scatter_dimension=0,...  105 us
    unnamed x2, blocking collectives  81.8 us
  transfers between devices with their start and end apart: 24, of which 16 were waited for; matrix products, arithmetic and copies ran while one was open for 43% of the time, Pallas kernels for 0%

commit v1 on v0

v1 whole, which is shorter than its diff:
```python
import jax
import jax.numpy as jnp
from jax import lax
from jax.experimental import pallas as pl
from jax.experimental.pallas import tpu as pltpu
from jax.sharding import PartitionSpec as P

MH = 24
HD = 64
NS = 128
QH = 8
KVH = 2
SSD_BLK = 128
ATT_BLK = 512


def product(form, left, right):
    return jnp.einsum(form, left, right, preferred_element_type=jnp.float32)


def matrix_product(form, left, right):
    return jnp.einsum(form, left, right, precision=lax.Precision.HIGHEST)


def rms_scale(values_in):
    return lax.rsqrt(jnp.mean(values_in * values_in, axis=-1, keepdims=True) + 1e-05)


def norm_back(values_in, scale_in, gain_in, grad_normed):
    weighted = grad_normed * gain_in
    grad_values = scale_in * weighted - values_in * scale_in**3 * jnp.mean(
        weighted * values_in, axis=-1, keepdims=True
    )
    grad_gain = jnp.sum(grad_normed * values_in * scale_in, axis=(0, 1))
    return (grad_values, grad_gain)


def rotate(vectors, positions, direction):
    half_dim = HD // 2
    frequency = 10000.0 ** (-(jnp.arange(half_dim, dtype=jnp.float32) * 2.0 / HD))
    angles = positions.astype(jnp.float32)[:, None] * frequency[None, :]
    cosine = jnp.cos(angles)[:, None, :]
    sine_part = direction * jnp.sin(angles)[:, None, :]
    first_half = vectors[..., :half_dim]
    second = vectors[..., half_dim:]
    return jnp.concatenate(
        [first_half * cosine - second * sine_part, second * cosine + first_half * sine_part],
        axis=-1,
    )


def exact_dot(left, right, left_dim, right_dim):
    return lax.dot_general(
        left,
        right,
        (((left_dim,), (right_dim,)), ((), ())),
        precision=lax.Precision.HIGHEST,
        preferred_element_type=jnp.float32,
    )


def low_half(rows):
    return lax.broadcasted_iota(jnp.int32, (rows, 2 * HD), 1) < HD


def spread_heads(per_head):
    rows, heads = per_head.shape
    lower = low_half(rows)
    return jnp.concatenate(
        [
            jnp.where(lower, per_head[:, h : h + 1], per_head[:, h + 1 : h + 2])
            for h in range(0, heads, 2)
        ],
        axis=1,
    )


def head_sums_of(wide):
    rows, width = wide.shape
    lower = low_half(rows)
    sums = []
    for start in range(0, width, 2 * HD):
        pair = wide[:, start : start + 2 * HD]
        sums.append(jnp.sum(jnp.where(lower, pair, 0.0), axis=1, keepdims=True))
        sums.append(jnp.sum(jnp.where(lower, 0.0, pair), axis=1, keepdims=True))
    return jnp.concatenate(sums, axis=1)


def split_pair(wide, start):
    pair = wide[:, start : start + 2 * HD]
    lower = low_half(pair.shape[0])
    return jnp.concatenate(
        [jnp.where(lower, pair, 0.0), jnp.where(lower, 0.0, pair)], axis=0
    )


def decay_of(cum, cum_row, h):
    blk = cum.shape[0]
    rows = lax.broadcasted_iota(jnp.int32, (blk, blk), 0)
    columns = lax.broadcasted_iota(jnp.int32, (blk, blk), 1)
    spread = cum[:, h : h + 1] - cum_row[h : h + 1, :]
    return jnp.exp(jnp.where(rows >= columns, spread, -1e30))


def scan_forward_kernel(
    x_ref, b_ref, c_ref, step_ref, cum_ref, step_row_ref, cum_row_ref, y_ref, kept_ref, state
):
    @pl.when(pl.program_id(1) == 0)
    def _():
        state[...] = jnp.zeros_like(state)

    x, bmat, cmat = x_ref[0], b_ref[0], c_ref[0]
    step, cum, step_row, cum_row = step_ref[0], cum_ref[0], step_row_ref[0], cum_row_ref[0]
    blk, heads = step.shape
    before = state[...]
    kept_ref[0, 0] = before
    inner = exact_dot(cmat, bmat, 1, 1)
    carried = exact_dot(cmat, before, 1, 0) * spread_heads(jnp.exp(cum))
    for h in range(0, heads, 2):
        mixing = jnp.concatenate(
            [inner * decay_of(cum, cum_row, k) * step_row[k : k + 1, :] for k in (h, h + 1)],
            axis=1,
        )
        columns = slice(h * HD, (h + 2) * HD)
        y_ref[0, :, columns] = (
            exact_dot(mixing, split_pair(x, h * HD), 1, 0) + carried[:, columns]
        )
    last = cum[blk - 1 :, :]
    fading = spread_heads(jnp.exp(last - cum) * step)
    state[...] = spread_heads(jnp.exp(last)) * before + exact_dot(bmat, fading * x, 0, 0)


def scan_backward_kernel(
    x_ref,
    b_ref,
    c_ref,
    step_ref,
    cum_ref,
    step_row_ref,
    cum_row_ref,
    kept_ref,
    up_ref,
    gx_ref,
    gb_ref,
    gc_ref,
    gstep_ref,
    gcum_ref,
    gstep_row_ref,
    gcum_row_ref,
    gstate,
):
    @pl.when(pl.program_id(1) == 0)
    def _():
        gstate[...] = jnp.zeros_like(gstate)

    x, bmat, cmat, up = x_ref[0], b_ref[0], c_ref[0], up_ref[0]
    step, cum, step_row, cum_row = step_ref[0], cum_ref[0], step_row_ref[0], cum_row_ref[0]
    blk, heads = step.shape
    before = kept_ref[0, 0]
    after = gstate[...]
    up_decayed = up * spread_heads(jnp.exp(cum))
    last = cum[blk - 1 :, :]
    weight = jnp.exp(last - cum)
    fading = weight * step
    fading_wide = spread_heads(fading)
    from_state = exact_dot(cmat, before, 1, 0)
    onto_x = exact_dot(bmat, after, 1, 0)
    grad_c = exact_dot(up_decayed, before, 1, 1)
    grad_b = exact_dot(fading_wide * x, after, 1, 1)
    meeting = head_sums_of(x * onto_x)
    gstep_ref[0] = weight * meeting
    leaving = fading * meeting
    end_part = jnp.sum(leaving, axis=0, keepdims=True) + jnp.exp(last) * head_sums_of(
        jnp.sum(after * before, axis=0, keepdims=True)
    )
    is_last = lax.broadcasted_iota(jnp.int32, (blk, heads), 0) == blk - 1
    grad_cum = (
        head_sums_of(up_decayed * from_state) - leaving + jnp.where(is_last, end_part, 0.0)
    )
    gstate[...] = spread_heads(jnp.exp(last)) * after + exact_dot(cmat, up_decayed, 0, 0)
    inner = exact_dot(cmat, bmat, 1, 1)
    grad_inner = jnp.zeros((blk, blk), jnp.float32)
    row_parts = []
    for h in range(0, heads, 2):
        columns = slice(h * HD, (h + 2) * HD)
        up_pair = split_pair(up, h * HD)
        grad_pair = exact_dot(up_pair, x[:, columns], 1, 1)
        mixings = []
        for k in (h, h + 1):
            decay = decay_of(cum, cum_row, k)
            row = step_row[k : k + 1, :]
            decayed = grad_pair[(k - h) * blk : (k - h + 1) * blk] * decay
            grad_inner += decayed * row
            both = decayed * inner
            row_sum = jnp.sum(both, axis=0, keepdims=True)
            gstep_row_ref[0, k : k + 1, :] = row_sum
            gcum_row_ref[0, k : k + 1, :] = -row_sum * row
            row_parts.append(jnp.sum(both * row, axis=1, keepdims=True))
            mixings.append(inner * decay * row)
        gx_ref[0, :, columns] = fading_wide[:, columns] * onto_x[:, columns] + exact_dot(
            jnp.concatenate(mixings, axis=0), up_pair, 0, 0
        )
    gcum_ref[0] = grad_cum + jnp.concatenate(row_parts, axis=1)
    gb_ref[0] = grad_b + exact_dot(grad_inner, cmat, 0, 0)
    gc_ref[0] = grad_c + exact_dot(grad_inner, bmat, 1, 0)


def scan_specs(heads, flip):
    def row_block(width):
        return pl.BlockSpec((1, SSD_BLK, width), lambda s, j: (s, flip(j), 0))

    across = pl.BlockSpec((1, heads, SSD_BLK), lambda s, j: (s, 0, flip(j)))
    kept = pl.BlockSpec((1, 1, NS, heads * HD), lambda s, j: (s, flip(j), 0, 0))
    return row_block, across, kept


def scan_call(body, ins, flip, backward):
    seqs, length, width = ins[0].shape
    heads = width // HD
    blocks = length // SSD_BLK
    row_block, across, kept = scan_specs(heads, flip)
    wide, state, slim = row_block(width), row_block(NS), row_block(heads)
    in_specs = [wide, state, state, slim, slim, across, across]

    def f32(*shape):
        return jax.ShapeDtypeStruct(shape, jnp.float32)

    if backward:
        in_specs = in_specs + [kept, wide]
        out_specs = [wide, state, state, slim, slim, across, across]
        out_shape = [
            f32(seqs, length, width),
            f32(seqs, length, NS),
            f32(seqs, length, NS),
            f32(seqs, length, heads),
            f32(seqs, length, heads),
            f32(seqs, heads, length),
            f32(seqs, heads, length),
        ]
    else:
        out_specs = [wide, kept]
        out_shape = [f32(seqs, length, width), f32(seqs, blocks, NS, width)]
    return pl.pallas_call(
        body,
        grid=(seqs, blocks),
        in_specs=in_specs,
        out_specs=out_specs,
        out_shape=out_shape,
        scratch_shapes=[pltpu.VMEM((NS, width), jnp.float32)],
        compiler_params=pltpu.CompilerParams(
            dimension_semantics=("arbitrary", "arbitrary"), vmem_limit_bytes=32 * 1024 * 1024
        ),
        cost_estimate=pl.CostEstimate(
            flops=20_000_000_000 if backward else 8_000_000_000,
            bytes_accessed=12_000_000,
            transcendentals=2_000_000,
        ),
    )(*ins)


def mamba_prepare(pre_conv, step_raw, conv_w, conv_b, log_rate, step_shift):
    seqs, length, _ = pre_conv.shape
    taps = conv_w.shape[1]
    heads = step_raw.shape[-1]
    padded = jnp.pad(pre_conv, ((0, 0), (taps - 1, 0), (0, 0)))
    conv_sum = conv_b[None, None, :]
    for offset in range(taps):
        conv_sum = conv_sum + padded[:, offset : offset + length] * conv_w[:, offset]
    activated = jax.nn.silu(conv_sum)
    step = jax.nn.softplus(step_raw + step_shift)
    logs = (step * -jnp.exp(log_rate)).reshape(seqs, length // SSD_BLK, SSD_BLK, heads)
    lower = jnp.tril(jnp.ones((SSD_BLK, SSD_BLK), jnp.float32))
    cum = matrix_product("ts,gbsh->gbth", lower, logs).reshape(seqs, length, heads)
    width = heads * HD
    return (
        activated[..., :width],
        activated[..., width : width + NS],
        activated[..., width + NS :],
        step,
        cum,
    )


def masked_scores(query_blk, key_seq, row_start, key_pos):
    scores = product("qhd,khd->hqk", query_blk, key_seq) * HD ** (-0.5)
    query_pos = row_start + jnp.arange(ATT_BLK)
    return jnp.where(key_pos[None, None, :] <= query_pos[None, :, None], scores, -jnp.inf)


def attend_forward(queries, key_rot, values):
    seq_count, length, head_count, _ = queries.shape
    blocks = length // ATT_BLK
    key_pos = jnp.arange(length)

    def one_block(flat_index):
        seq_index = flat_index // blocks
        row_start = flat_index % blocks * ATT_BLK
        query_blk = lax.dynamic_slice(
            queries, (seq_index, row_start, 0, 0), (1, ATT_BLK, head_count, HD)
        )[0]
        key_seq = lax.dynamic_index_in_dim(key_rot, seq_index, 0, keepdims=False)
        value_seq = lax.dynamic_index_in_dim(values, seq_index, 0, keepdims=False)
        scores = masked_scores(query_blk, key_seq, row_start, key_pos)
        row_peak = jnp.max(scores, axis=-1, keepdims=True)
        raised = jnp.exp(scores - row_peak)
        totals = jnp.sum(raised, axis=-1, keepdims=True)
        attn_probs = raised / totals
        output = product("hqk,khd->qhd", attn_probs.astype(jnp.bfloat16), value_seq)
        return (output, row_peak[..., 0] + jnp.log(totals[..., 0]))

    output_values, logsum = lax.map(one_block, jnp.arange(seq_count * blocks))
    return (
        output_values.reshape(seq_count, length, head_count, HD),
        logsum.reshape(seq_count, blocks, head_count, ATT_BLK),
    )


def attend_backward(queries, key_rot, values, logsum, grad_out):
    seq_count, length, head_count, _ = queries.shape
    blocks = length // ATT_BLK
    key_pos = jnp.arange(length)
    score_scale = HD ** (-0.5)

    def attend_one_seq(operands):
        query_seq, key_seq, value_seq, logsum_seq, grad_seq = operands

        def one_move_forward(running, blk_index):
            grad_keys_acc, grad_values_acc = running
            row_start = blk_index * ATT_BLK
            query_blk = lax.dynamic_slice_in_dim(query_seq, row_start, ATT_BLK, 0)
            grad_blk = lax.dynamic_slice_in_dim(grad_seq, row_start, ATT_BLK, 0)
            scores = masked_scores(query_blk, key_seq, row_start, key_pos)
            attn_probs = jnp.exp(
                scores
                - lax.dynamic_index_in_dim(logsum_seq, blk_index, 0, keepdims=False)[:, :, None]
            )
            probs_low = attn_probs.astype(jnp.bfloat16)
            grad_probs = product("qhd,khd->hqk", grad_blk, value_seq)
            offset_mean = jnp.sum(attn_probs * grad_probs, axis=-1, keepdims=True)
            grad_scores = (attn_probs * (grad_probs - offset_mean)).astype(jnp.bfloat16)
            grad_query_blk = product("hqk,khd->qhd", grad_scores, key_seq) * score_scale
            grad_keys_acc = (
                grad_keys_acc + product("hqk,qhd->khd", grad_scores, query_blk) * score_scale
            )
            grad_values_acc = grad_values_acc + product("hqk,qhd->khd", probs_low, grad_blk)
            return ((grad_keys_acc, grad_values_acc), grad_query_blk)

        zeros_kv = jnp.zeros((length, head_count, HD), jnp.float32)
        (grad_keys_seq, grad_values_seq), grad_query_blocks = lax.scan(
            one_move_forward, (zeros_kv, zeros_kv), jnp.arange(blocks)
        )
        return (grad_query_blocks.reshape(length, head_count, HD), grad_keys_seq, grad_values_seq)

    return lax.map(attend_one_seq, (queries, key_rot, values, logsum, grad_out))


def pair_half(parts, axis_name, dim, place, count):
    idx = lax.axis_index(axis_name)
    bit = (idx // place) % 2
    kept = lax.dynamic_index_in_dim(parts, bit, dim, keepdims=False)
    given = lax.dynamic_index_in_dim(parts, 1 - bit, dim, keepdims=False)
    got = lax.ppermute(given, axis_name, [(i, i ^ place) for i in range(count)])
    return kept.astype(jnp.float32) + got.astype(jnp.float32)


def scatter_sum(parts, axes, rows_first=False):
    bits = []
    for name in axes:
        count = lax.axis_size(name)
        place = count // 2
        while place:
            bits.append((name, place, count))
            place //= 2
    shape = parts.shape[1:]
    parts = parts.reshape((2,) * len(bits) + shape)
    near = [bit for bit in bits if bit[0] == "ctx"][::-1]
    rows = [bit for bit in bits if bit[0] == "fsdp"]
    order = near[:1] + rows + near[1:] if rows_first else near + rows
    order = order + [bit for bit in bits if bit[0] == "tp"]
    left = list(bits)
    for bit in order:
        dim = left.index(bit)
        parts = pair_half(parts.astype(jnp.bfloat16), bit[0], dim, bit[1], bit[2])
        left.remove(bit)
    return parts.reshape(shape)


def butterfly_sum(value, axes):
    for name in axes:
        count = lax.axis_size(name)
        place = 1
        while place < count:
            value = value + lax.ppermute(value, name, [(i, i ^ place) for i in range(count)])
            place *= 2
    return value


def line_gather(value, name):
    count = lax.axis_size(name)
    here = lax.axis_index(name)
    up, down = [value], [value]
    for _ in range(count - 1):
        up.append(lax.ppermute(up[-1], name, [(i, i + 1) for i in range(count - 1)]))
        down.append(lax.ppermute(down[-1], name, [(i + 1, i) for i in range(count - 1)]))
    blocks = []
    for owner in range(count):
        block = value
        for away in range(1, count):
            block = jnp.where(here - owner == away, up[away], block)
            block = jnp.where(owner - here == away, down[away], block)
        blocks.append(block)
    return jnp.concatenate(blocks, axis=0)


def on_device(
    tokens,
    cotangent,
    mixer_gain,
    mixer_input_weight,
    step_weight,
    query_key_value_weight,
    conv_weight,
    conv_bias,
    a_log,
    step_bias,
    skip_gain,
    mixer_output_weight,
    attention_output_weight,
    mlp_gain,
    gate_up_weight,
    down_weight,
):
    seq_count, local_len, _ = tokens.shape
    ctx_size = lax.axis_size("ctx")
    ctx_index = lax.axis_index("ctx")
    mamba_width = MH * HD
    heads_dev = MH // ctx_size
    query_dev = QH // ctx_size
    x_dev = heads_dev * HD
    q_dev = query_dev * HD
    full_len = local_len * ctx_size

    devices_axes = ("fsdp", "ctx", "tp")
    zx_cols = mixer_input_weight.shape[1]
    qkv_cols = query_key_value_weight.shape[1]
    packed_cols = -(-(zx_cols + qkv_cols + MH + 2) // 128) * 128
    in_packed = jnp.concatenate(
        [
            mixer_input_weight,
            query_key_value_weight,
            step_weight,
            mixer_gain[:, None],
            mlp_gain[:, None],
            jnp.zeros(
                (mixer_gain.shape[0], packed_cols - zx_cols - qkv_cols - MH - 2), jnp.bfloat16
            ),
        ],
        axis=1,
    )
    in_full = lax.all_gather(in_packed, devices_axes, axis=0, tiled=True)
    zx_full = in_full[:, :zx_cols]
    qkv_full = in_full[:, zx_cols : zx_cols + qkv_cols]
    step_full = in_full[:, zx_cols + qkv_cols : zx_cols + qkv_cols + MH]
    gain_one = in_full[:, zx_cols + qkv_cols + MH]
    gain_two = in_full[:, zx_cols + qkv_cols + MH + 1]
    out_rows = mixer_output_weight.shape[0]
    out_packed = jnp.concatenate([mixer_output_weight, attention_output_weight], axis=0)
    out_full = lax.all_gather(out_packed, devices_axes, axis=0)
    gate_up_full = lax.all_gather(gate_up_weight, ("fsdp", "ctx"), axis=0, tiled=True)
    down_full = lax.all_gather(down_weight, ("fsdp", "ctx"), axis=0, tiled=True)
    cot_all = line_gather(cotangent, "tp")
    tokens_f = tokens.astype(jnp.float32)
    scale_one = rms_scale(tokens_f)
    first_normalized = (tokens_f * scale_one * gain_one.astype(jnp.float32)).astype(jnp.bfloat16)
    mixer_input_projection = product("gld,de->gle", first_normalized, zx_full)
    step_projection = product("gld,de->gle", first_normalized, step_full).astype(jnp.bfloat16)
    query_key_value_projection = product("gld,de->gle", first_normalized, qkv_full).astype(
        jnp.bfloat16
    )
    gate_z = mixer_input_projection[..., :mamba_width]
    conv_in = mixer_input_projection[..., mamba_width:].astype(jnp.bfloat16)
    group = QH // KVH
    kv_dev = max(query_dev // group, 1)
    kv_copies = kv_dev * ctx_size // KVH
    kv_cols = kv_dev * HD
    send_cols = x_dev + q_dev + 2 * NS + 2 * kv_cols
    step_cols = -(send_cols + heads_dev) % 128 + heads_dev

    def to_heads(rows):
        pieces = rows.reshape(seq_count, local_len, ctx_size, -1)
        return jnp.transpose(pieces, (2, 0, 1, 3))

    def to_all(rows):
        return jnp.broadcast_to(rows[None], (ctx_size,) + rows.shape)

    def exchange(pieces):
        return lax.all_to_all(pieces, "ctx", split_axis=0, concat_axis=0, tiled=True)

    def to_sequence(pieces):
        return jnp.transpose(pieces, (1, 0, 2, 3)).reshape(seq_count, full_len, -1)

    def to_parts(rows):
        return jnp.transpose(
            rows.reshape(seq_count, ctx_size, local_len, rows.shape[-1]), (1, 0, 2, 3)
        )

    def join_heads(pieces):
        return jnp.transpose(pieces, (1, 2, 0, 3)).reshape(seq_count, local_len, -1)

    def kv_pieces(rows):
        heads = jnp.repeat(rows.reshape(seq_count, local_len, KVH, HD), kv_copies, axis=2)
        return to_heads(heads)

    heads_send = jnp.concatenate(
        [
            to_heads(conv_in[..., :mamba_width]),
            to_heads(query_key_value_projection[..., : QH * HD]),
            to_all(conv_in[..., mamba_width:]),
            kv_pieces(query_key_value_projection[..., QH * HD : (QH + KVH) * HD]),
            kv_pieces(query_key_value_projection[..., (QH + KVH) * HD :]),
            to_heads(step_projection),
            jnp.zeros(
                (ctx_size, seq_count, local_len, step_cols - heads_dev), jnp.bfloat16
            ),
        ],
        axis=-1,
    )
    heads_send, cot_all = lax.optimization_barrier((heads_send, cot_all))
    heads_in = to_sequence(exchange(heads_send))
    bc_start = x_dev + q_dev
    key_start = bc_start + 2 * NS
    value_start = key_start + kv_cols
    step_heads = heads_in[..., send_cols : send_cols + heads_dev]
    conv_rows = jnp.concatenate(
        [
            lax.dynamic_slice_in_dim(conv_weight, ctx_index * x_dev, x_dev, 0),
            conv_weight[mamba_width:],
        ],
        axis=0,
    ).astype(jnp.float32)
    bias_rows = jnp.concatenate(
        [lax.dynamic_slice_in_dim(conv_bias, ctx_index * x_dev, x_dev, 0), conv_bias[mamba_width:]],
        axis=0,
    ).astype(jnp.float32)
    rate_rows = lax.dynamic_slice_in_dim(a_log, ctx_index * heads_dev, heads_dev, 0).astype(
        jnp.float32
    )
    shift_rows = lax.dynamic_slice_in_dim(step_bias, ctx_index * heads_dev, heads_dev, 0).astype(
        jnp.float32
    )
    skip_rows = lax.dynamic_slice_in_dim(skip_gain, ctx_index * heads_dev, heads_dev, 0).astype(
        jnp.float32
    )
    mamba_in = jnp.concatenate(
        [heads_in[..., :x_dev], heads_in[..., bc_start:key_start]], axis=-1
    ).astype(jnp.float32)
    (scan_x, scan_b, scan_c, scan_step, scan_cum), prepare_pull = jax.vjp(
        mamba_prepare,
        mamba_in,
        step_heads.astype(jnp.float32),
        conv_rows,
        bias_rows,
        rate_rows,
        shift_rows,
    )
    scan_ins = (
        scan_x,
        scan_b,
        scan_c,
        scan_step,
        scan_cum,
        jnp.swapaxes(scan_step, 1, 2),
        jnp.swapaxes(scan_cum, 1, 2),
    )
    scan_y, scan_kept = scan_call(scan_forward_kernel, scan_ins, lambda j: j, False)
    skip_wide = jnp.repeat(skip_rows, HD)
    mamba_out = scan_y + skip_wide * scan_x
    positions = jnp.arange(full_len)
    queries = rotate(
        heads_in[..., x_dev:bc_start].astype(jnp.float32).reshape(
            seq_count, full_len, query_dev, HD
        ),
        positions,
        1.0,
    ).astype(jnp.bfloat16)
    key_rot = rotate(
        heads_in[..., key_start:value_start].astype(jnp.float32).reshape(
            seq_count, full_len, kv_dev, HD
        ),
        positions,
        1.0,
    ).astype(jnp.bfloat16)
    values = heads_in[..., value_start:send_cols].reshape(seq_count, full_len, kv_dev, HD)
    key_rot = jnp.repeat(key_rot, query_dev // kv_dev, axis=2)
    values = jnp.repeat(values, query_dev // kv_dev, axis=2)
    attn_out, logsum = attend_forward(queries, key_rot, values)
    back_send = jnp.concatenate(
        [
            mamba_out.astype(jnp.bfloat16),
            attn_out.reshape(seq_count, full_len, q_dev).astype(jnp.bfloat16),
        ],
        axis=-1,
    )
    back_send, out_full, gate_up_full, down_full = lax.optimization_barrier(
        (back_send, out_full, gate_up_full, down_full)
    )
    mamba_proj = out_full[:, :out_rows].reshape(mamba_width, -1)
    attn_proj = out_full[:, out_rows:].reshape(QH * HD, -1)
    back_tokens = exchange(to_parts(back_send))
    mamba_tok = join_heads(back_tokens[..., :x_dev])
    attn_tok = join_heads(back_tokens[..., x_dev:])
    sig_z = jax.nn.sigmoid(gate_z)
    silu_z = gate_z * sig_z
    gated_mixture = (mamba_tok.astype(jnp.float32) * silu_z).astype(jnp.bfloat16)
    branch_output = product("gle,ed->gld", gated_mixture, mamba_proj) + product(
        "gle,ed->gld", attn_tok, attn_proj
    )
    residual_stream = tokens_f + branch_output
    scale_two = rms_scale(residual_stream)
    second_normalized = (residual_stream * scale_two * gain_two.astype(jnp.float32)).astype(
        jnp.bfloat16
    )
    rows_all = lax.all_gather(second_normalized, "tp", axis=0, tiled=True)
    gate_up_values = product("gld,dcf->glcf", rows_all, gate_up_full)
    gate_part = gate_up_values[..., 0, :]
    up_part = gate_up_values[..., 1, :]
    sig_gate = jax.nn.sigmoid(gate_part)
    silu_gate = gate_part * sig_gate
    hidden_units = (silu_gate * up_part).astype(jnp.bfloat16)
    partial_out = product("glf,df->gld", hidden_units, down_full)
    mlp_out = lax.psum_scatter(
        partial_out.astype(jnp.bfloat16), "tp", scatter_dimension=0, tiled=True
    ).astype(jnp.float32)
    out_block = (residual_stream + mlp_out).astype(jnp.bfloat16)
    grad_hidden = product("gld,df->glf", cot_all, down_full)
    grad_down = product("gld,glf->df", cot_all, hidden_units)
    slope_gate = sig_gate * (1.0 + gate_part * (1.0 - sig_gate))
    grad_gate_up = jnp.stack(
        [grad_hidden * up_part * slope_gate, grad_hidden * silu_gate], axis=2
    ).astype(jnp.bfloat16)
    grad_gu_w = product("gld,glcf->dcf", rows_all, grad_gate_up)
    grad_rows_part = product("glcf,dcf->gld", grad_gate_up, gate_up_full)
    grad_normed_two = lax.psum_scatter(
        grad_rows_part.astype(jnp.bfloat16), "tp", scatter_dimension=0, tiled=True
    ).astype(jnp.float32)
    grad_residual, grad_gain_two = norm_back(
        residual_stream, scale_two, gain_two.astype(jnp.float32), grad_normed_two
    )
    grad_residual = grad_residual + cotangent.astype(jnp.float32)
    grad_branch = grad_residual.astype(jnp.bfloat16)
    grad_mamba_proj = product("gle,gld->ed", gated_mixture, grad_branch)
    grad_attn_proj = product("gle,gld->ed", attn_tok, grad_branch)
    grad_gated = product("gld,ed->gle", grad_branch, mamba_proj)
    slope_z = sig_z * (1.0 + gate_z * (1.0 - sig_z))
    grad_mamba_tok = (grad_gated * silu_z).astype(jnp.bfloat16)
    grad_z = grad_gated * mamba_tok.astype(jnp.float32) * slope_z
    grad_attn_tok = product("gld,ed->gle", grad_branch, attn_proj).astype(jnp.bfloat16)
    out_sums = scatter_sum(
        jnp.concatenate(
            [
                grad_mamba_proj.reshape(-1, out_rows, grad_mamba_proj.shape[1]),
                grad_attn_proj.reshape(
                    -1, attention_output_weight.shape[0], grad_attn_proj.shape[1]
                ),
            ],
            axis=1,
        ).astype(jnp.bfloat16),
        devices_axes,
    )
    gate_up_sum = scatter_sum(
        grad_gu_w.astype(jnp.bfloat16).reshape((-1,) + gate_up_weight.shape), ("fsdp", "ctx")
    )
    down_sum = scatter_sum(
        grad_down.astype(jnp.bfloat16).reshape((-1,) + down_weight.shape), ("fsdp", "ctx")
    )
    grad_heads = to_sequence(
        exchange(
            jnp.concatenate([to_heads(grad_mamba_tok), to_heads(grad_attn_tok)], axis=-1)
        )
    )
    grad_mamba = grad_heads[..., :x_dev].astype(jnp.float32)
    gx, gb, gc, gstep, gcum, gstep_row, gcum_row = scan_call(
        scan_backward_kernel,
        scan_ins + (scan_kept, grad_mamba),
        lambda j: full_len // SSD_BLK - 1 - j,
        True,
    )
    grad_skip = jnp.sum(
        (grad_mamba * scan_x).reshape(-1, heads_dev, HD), axis=(0, 2)
    )
    grad_pre, grad_step, grad_conv_w, grad_conv_b, grad_rate, grad_shift = prepare_pull(
        (
            gx + skip_wide * grad_mamba,
            gb,
            gc,
            gstep + jnp.swapaxes(gstep_row, 1, 2),
            gcum + jnp.swapaxes(gcum_row, 1, 2),
        )
    )
    grad_queries, grad_keys, grad_values = attend_backward(
        queries,
        key_rot,
        values,
        logsum,
        grad_heads[..., x_dev:].reshape(seq_count, full_len, query_dev, HD),
    )
    grad_queries = rotate(grad_queries, positions, -1.0)
    grad_keys = jnp.sum(
        grad_keys.reshape(seq_count, full_len, kv_dev, query_dev // kv_dev, HD), axis=3
    )
    grad_values = jnp.sum(
        grad_values.reshape(seq_count, full_len, kv_dev, query_dev // kv_dev, HD), axis=3
    )
    grad_keys = rotate(grad_keys, positions, -1.0)
    tokens_send = jnp.concatenate(
        [
            grad_pre[..., :x_dev],
            grad_queries.reshape(seq_count, full_len, q_dev),
            grad_pre[..., x_dev:],
            grad_keys.reshape(seq_count, full_len, kv_cols),
            grad_values.reshape(seq_count, full_len, kv_cols),
            grad_step,
            jnp.zeros((seq_count, full_len, step_cols - heads_dev), jnp.float32),
        ],
        axis=-1,
    ).astype(jnp.bfloat16)
    tokens_send, out_sums, gate_up_sum, down_sum, out_block = lax.optimization_barrier(
        (tokens_send, out_sums, gate_up_sum, down_sum, out_block)
    )
    tokens_back = exchange(to_parts(tokens_send))
    grad_x_conv = join_heads(tokens_back[..., :x_dev])
    grad_query_tok = join_heads(tokens_back[..., x_dev:bc_start])
    grad_bc = jnp.sum(tokens_back[..., bc_start:key_start].astype(jnp.float32), axis=0)

    def kv_sum(pieces):
        joined = join_heads(pieces).astype(jnp.float32)
        return jnp.sum(
            joined.reshape(seq_count, local_len, KVH, kv_copies, HD), axis=3
        ).reshape(seq_count, local_len, KVH * HD)

    grad_key_tok = kv_sum(tokens_back[..., key_start:value_start])
    grad_value_tok = kv_sum(tokens_back[..., value_start:send_cols])
    step_tok = join_heads(tokens_back[..., send_cols : send_cols + heads_dev])
    grad_zx = jnp.concatenate([grad_z.astype(jnp.bfloat16), grad_x_conv, grad_bc.astype(jnp.bfloat16)], axis=-1)
    grad_step_low = step_tok
    grad_qkv = jnp.concatenate(
        [
            grad_query_tok,
            grad_key_tok.astype(jnp.bfloat16),
            grad_value_tok.astype(jnp.bfloat16),
        ],
        axis=-1,
    )
    grad_normed_one = (
        product("gle,de->gld", grad_zx, zx_full)
        + product("gle,de->gld", grad_step_low, step_full)
        + product("gle,de->gld", grad_qkv, qkv_full)
    )
    grad_zx_w = product("gld,gle->de", first_normalized, grad_zx)
    grad_step_w = product("gld,gle->de", first_normalized, grad_step_low)
    grad_qkv_w = product("gld,gle->de", first_normalized, grad_qkv)
    grad_input, grad_gain_one = norm_back(
        tokens_f, scale_one, gain_one.astype(jnp.float32), grad_normed_one
    )
    grad_input = grad_input + grad_residual
    in_grads = (
        jnp.concatenate([grad_zx_w, grad_qkv_w, grad_step_w], axis=1)
        .astype(jnp.bfloat16)
        .reshape(-1, mixer_gain.shape[0], zx_cols + qkv_cols + MH)
    )
    middle = (zx_cols + qkv_cols) // 2
    in_sums = jnp.concatenate(
        [
            scatter_sum(in_grads[..., :middle], devices_axes),
            scatter_sum(in_grads[..., middle:], devices_axes, True),
        ],
        axis=-1,
    )
    conv_full = jnp.concatenate(
        [
            lax.dynamic_update_slice_in_dim(
                jnp.zeros((mamba_width, grad_conv_w.shape[1]), jnp.float32),
                grad_conv_w[:x_dev],
                ctx_index * x_dev,
                0,
            ),
            grad_conv_w[x_dev:],
        ],
        axis=0,
    )
    bias_full = jnp.concatenate(
        [
            lax.dynamic_update_slice_in_dim(
                jnp.zeros((mamba_width,), jnp.float32), grad_conv_b[:x_dev], ctx_index * x_dev, 0
            ),
            grad_conv_b[x_dev:],
        ],
        axis=0,
    )
    rate_full = lax.dynamic_update_slice_in_dim(
        jnp.zeros((MH,), jnp.float32), grad_rate, ctx_index * heads_dev, 0
    )
    shift_full = lax.dynamic_update_slice_in_dim(
        jnp.zeros((MH,), jnp.float32), grad_shift, ctx_index * heads_dev, 0
    )
    skip_full = lax.dynamic_update_slice_in_dim(
        jnp.zeros((MH,), jnp.float32), grad_skip, ctx_index * heads_dev, 0
    )
    flat_parts = [
        conv_full.T.reshape(-1),
        bias_full,
        rate_full,
        shift_full,
        skip_full,
        grad_gain_one,
        grad_gain_two,
    ]
    sizes = [part.shape[0] for part in flat_parts]
    total = sum(sizes)
    flat = jnp.concatenate(flat_parts + [jnp.zeros((-total % 1024,), jnp.float32)])
    flat = butterfly_sum(flat.reshape(-1, 128), devices_axes).reshape(-1)
    head_sums = []
    start = 0
    for size in sizes:
        head_sums.append(flat[start : start + size])
        start += size
    gain_rows = mixer_gain.shape[0]
    place = lax.axis_index(devices_axes) * gain_rows
    return (
        out_block,
        grad_input.astype(jnp.bfloat16),
        lax.dynamic_slice_in_dim(head_sums[5], place, gain_rows, 0),
        in_sums[:, :zx_cols],
        in_sums[:, zx_cols + qkv_cols :],
        in_sums[:, zx_cols : zx_cols + qkv_cols],
        head_sums[0].reshape(conv_full.shape[1], conv_full.shape[0]).T,
        head_sums[1],
        head_sums[2],
        head_sums[3],
        head_sums[4],
        out_sums[:out_rows],
        out_sums[out_rows:],
        lax.dynamic_slice_in_dim(head_sums[6], place, gain_rows, 0),
        gate_up_sum,
        down_sum,
    )


def solution(mesh):
    placed = (
        P(("fsdp", "tp"), "ctx", None),
        P(("fsdp", "tp"), "ctx", None),
        P(("fsdp", "ctx", "tp")),
        P(("fsdp", "ctx", "tp"), None),
        P(("fsdp", "ctx", "tp"), None),
        P(("fsdp", "ctx", "tp"), None),
        P(),
        P(),
        P(),
        P(),
        P(),
        P(("fsdp", "ctx", "tp"), None),
        P(("fsdp", "ctx", "tp"), None),
        P(("fsdp", "ctx", "tp")),
        P(("fsdp", "ctx"), None, "tp"),
        P(("fsdp", "ctx"), "tp"),
    )
    return jax.shard_map(
        on_device,
        mesh=mesh,
        in_specs=placed,
        out_specs=(
            P(("fsdp", "tp"), "ctx", None),
            P(("fsdp", "tp"), "ctx", None),
            P(("fsdp", "ctx", "tp")),
            P(("fsdp", "ctx", "tp"), None),
            P(("fsdp", "ctx", "tp"), None),
            P(("fsdp", "ctx", "tp"), None),
            P(),
            P(),
            P(),
            P(),
            P(),
            P(("fsdp", "ctx", "tp"), None),
            P(("fsdp", "ctx", "tp"), None),
            P(("fsdp", "ctx", "tp")),
            P(("fsdp", "ctx"), None, "tp"),
            P(("fsdp", "ctx"), "tp"),
        ),
        check_vma=False,
    )
```

time: 2010 us -> 777 us (0.39)
  waiting for transfers between devices: 881 us -> 339 us
  local copies, waits for them, and re-layouts: 410 us -> 118 us
  matrix products: 295 us -> 98 us
  blocking collectives: 157 us -> 0 us
  other arithmetic: 195 us -> 98.7 us
  starting transfers between devices: 29 us -> 61 us
  Pallas kernels: 0 us -> 28.1 us
    reduce_scatter x6 -> x0, waiting for transfers between devices: 667 us -> none  [the longest x1 297 us: on_device(): lax.psum_scatter(grad_zx_w, ('fsdp', 'ctx', 'tp'), scatter_dimension=0, t...]
    dot_general x120 -> x2, matrix products: 186 us -> 1.13 us  [matrix_product(): return jnp.einsum(form, left, right, precision=lax.Precision.HIGHEST)]
    ppermute x0 -> x32, waiting for transfers between devices: none -> 138 us  [the longest x21 87.9 us: pair_half(): got = lax.ppermute(given, axis_name, [(i, i ^ place) for i in range(count)])]
    dynamic_update_slice x104 -> x0, local copies, waits for them, and re-layouts: 135 us -> none  [state_scan(): lax.scan(state_move_forward, initial_state, (regroup_blocks(input_values)...]
    unnamed x2 -> x0, blocking collectives: 81.8 us -> none
    all_gather x1 -> x0, blocking collectives: 68.7 us -> none  [gather_mixer(): lax.all_gather(step_weight, ('fsdp', 'ctx', 'tp'), axis=0, tiled=True)]
    ppermute x0 -> x32, starting transfers between devices: none -> 44.7 us  [the longest x21 18.5 us: pair_half(): got = lax.ppermute(given, axis_name, [(i, i ^ place) for i in range(count)])]
    reduce_scatter x1, waiting for transfers between devices: 0.01 us -> 44.4 us  [on_device(): lax.psum_scatter(partial_out.astype(jnp.bfloat16), 'tp', scatter_dimensio...]
  transfers between devices with their start and end apart: 24 -> 43, of which waited for: 16 -> 31; matrix products, arithmetic and copies ran while one was open for 43% -> 29% of each run, Pallas kernels for 0% -> 4%
where the time goes in v1:
time: 777 us; the launch traced here: 769 us
  waiting for transfers between devices  339 us (44%)
  local copies, waits for them, and re-layouts  118 us (15%)
  other arithmetic  98.7 us (13%)
  matrix products  98 us (13%)
  starting transfers between devices  61 us (8%)
  Pallas kernels  28.1 us (4%)
  between operations  16.9 us (2%)
  loops' own time  9.42 us (1%)
    dot_general x35, matrix products, product(): return jnp.einsum(form, left, right, preferred_element_type=jnp.float32)  96.9 us
    ppermute x21, waiting for transfers between devices, pair_half(): got = lax.ppermute(given, axis_name, [(i, i ^ place) for i in range(count)])  87.9 us
    all_to_all x4, waiting for transfers between devices, exchange(): lax.all_to_all(pieces, 'ctx', split_axis=0, concat_axis=0, tiled=True)  63 us
    reduce_scatter x1, waiting for transfers between devices, on_device(): lax.psum_scatter(partial_out.astype(jnp.bfloat16), 'tp', scatter_dimensio...  44.4 us
    all_gather x1, waiting for transfers between devices, on_device(): rows_all = lax.all_gather(second_normalized, 'tp', axis=0, tiled=True)  44.4 us
    ppermute x3, waiting for transfers between devices, line_gather(): lax.ppermute(down[-1], name, [(i + 1, i) for i in range(count - 1)])  29.8 us
    pallas_call x2, Pallas kernels, scan_call(): pl.pallas_call(body, grid=(seqs, blocks), in_specs=in_specs, out_specs=ou...  28.1 us
    unnamed x280, local copies, waits for them, and re-layouts  27.3 us
  transfers between devices with their start and end apart: 43, of which 31 were waited for; matrix products, arithmetic and copies ran while one was open for 29% of the time, Pallas kernels for 4%

profile of v1, /device:TPU:0, one launch (start us, length us, event | category | flops | bytes accessed | tf_op | source)
XLA Modules:
  0.0 768.9 jit_solution(14832091609763383950)
XLA Ops:
  13.4 5.6 collective-permute-start.3
  19.0 12.9 %collective-permute-done = bf16[1,256,1024]{2,1,0:T(8,128)(2,1)S(1)} collective-permute-done((bf16[1,256,1024]{2,1,0:T(8,128)(2,1)}, bf16[1,256,1024]{2,1,0:T(8,128)(2,1)S(1)}, u32[]{:S(2)}, u32[]{:S(2)}) %collective-permute-start) | collective-permute-done | bytes 524320 | tf_op jit(solution)/shard_map/ppermute | solution.py:404
  36.2 4.3 collective-permute-start.4
  40.5 13.8 %collective-permute-done.1 = bf16[1,256,1024]{2,1,0:T(8,128)(2,1)S(1)} collective-permute-done((bf16[1,256,1024]{2,1,0:T(8,128)(2,1)S(1)}, bf16[1,256,1024]{2,1,0:T(8,128)(2,1)S(1)}, u32[]{:S(2)}, u32[]{:S(2)}) %collective-permute-start.1) | collective-permute-done | bytes 524320 | tf_op jit(solution)/shard_map/ppermute | solution.py:404
  55.6 5.3 collective-permute-done.4
  61.0 4.4 collective-permute-start.5
  70.4 4.9 collective-permute-done.5
  78.5 23.7 %all-gather.7.cloned.1.call-done = bf16[1024,4224]{1,0:T(8,128)(2,1)} async-done(((bf16[32,4224]{1,0:T(8,128)(2,1)}), bf16[1024,4224]{1,0:T(8,128)(2,1)}) %all-gather.7.cloned.1.call-update) | async-done | bytes 8650768 | tf_op jit(solution)/shard_map/all_gather | solution.py:460
  103.6 6.6 fusion.205
  116.1 3.9 concatenate.127
  120.0 3.8 all-to-all-start
  128.0 24.3 %all-to-all-done = bf16[4,1,256,1024]{3,2,1,0:T(8,128)(2,1)S(1)} async-done(((bf16[4,1,256,1024]{3,2,1,0:T(8,128)(2,1)}), bf16[4,1,256,1024]{3,2,1,0:T(8,128)(2,1)S(1)}, u32[]{:S(2)}, u32[]{:S(2)}) %all-to-all-start) | async-done | bytes 2097184 | tf_op jit(solution)/shard_map/all_to_all | solution.py:497
  164.9 18.3 %while.41 = (s32[]{:T(128)}, bf16[2,512,2,64]{1,3,2,0:T(8,128)(2,1)}, f32[2,2,512]{2,1,0:T(2,128)S(1)}, s32[2]{0:T(128)S(1)}, bf16[1,1024,2,64]{1,3,2,0:T(8,128)...) while((s32[]{:T(128)}, ...), condition=%wide.region_4.5_spmd.clone, body=%wide.region_1.4_spmd.clone.sunk | while | flops 281542144 | bytes 17469804 | solution.py:311
  191.5 8.8 %shard_map.279 = (f32[1,1024,384]{2,1,0:T(8,128)S(1)}, f32[1,8,128,384]{3,2,1,0:T(8,128)S(1)}) custom-call(f32[1,1024,384]{2,1,0:T(8,128)S(1)} %slice.326.x_ref, f32[1,1024,128]{2,1,0:T(8,128)S(1)} %get-tuple-element.554.b_ref, f32[1,1024,128]{2,1,0:T(8,128)S(1)} %get-tuple-element.553.c_ref, f32[1,1024,6]{2,1,0:T(8,128)S(1)} %get-tuple-element.557.step_ref, ...), custom_call_target="tpu_custom_call" | custom-call | flops 8000000000 | bytes 12000000 | tf_op jit(solution)/shard_map/pallas_call | solution.py:243
  201.7 24.9 %all-gather.15.cloned.1.call-done = bf16[2048,1024]{1,0:T(8,128)(2,1)} async-done(((bf16[64,1024]{1,0:T(8,128)(2,1)}), bf16[2048,1024]{1,0:T(8,128)(2,1)}) %all-gather.15.cloned.1.call-update) | async-done | bytes 4194320 | tf_op jit(solution)/shard_map/all_gather | solution.py:468
  227.8 4.2 all-to-all-start.1
  234.7 4.1 slice.270
  238.8 7.8 %all-to-all-done.1 = bf16[4,1,256,512]{2,3,1,0:T(8,128)(2,1)} async-done(((bf16[4,1,256,512]{2,3,1,0:T(8,128)(2,1)}), bf16[4,1,256,512]{2,3,1,0:T(8,128)(2,1)}, u32[]{:S(2)}, u32[]{:S(2)}) %all-to-all-start.1) | async-done | bytes 1048608 | tf_op jit(solution)/shard_map/all_to_all | solution.py:497
  256.6 44.4 %all-gather.13.cloned.1.call-done = bf16[4,256,1024]{2,1,0:T(8,128)(2,1)} async-done(((bf16[1,256,1024]{2,1,0:T(8,128)(2,1)}), bf16[4,256,1024]{2,1,0:T(8,128)(2,1)}) %all-gather.13.cloned.1.call-update) | async-done | bytes 2097168 | tf_op jit(solution)/shard_map/all_gather | solution.py:623
  301.0 4.7 fusion.75
  310.1 3.7 bitcast_convert_fusion.1
  314.3 4.2 convolution_convert_fusion.2
  318.5 4.6 bitcast_convert_fusion
  357.8 44.4 %reduce-scatter.5.cloned.1.call-done = bf16[1,256,1024]{2,1,0:T(8,128)(2,1)} async-done(((bf16[4,256,1024]{2,1,0:T(8,128)(2,1)}), bf16[1,256,1024]{2,1,0:T(8,128)(2,1)}) %reduce-scatter.5.cloned.1.call-update) | async-done | bytes 524304 | tf_op jit(solution)/shard_map/reduce_scatter | solution.py:631
  405.7 4.0 fusion.82
  421.7 8.0 %all-to-all-done.2 = bf16[4,1,256,512]{3,2,1,0:T(8,128)(2,1)S(1)} async-done(((bf16[4,1,256,512]{3,2,1,0:T(8,128)(2,1)}), bf16[4,1,256,512]{3,2,1,0:T(8,128)(2,1)S(1)}, u32[]{:S(2)}, u32[]{:S(2)}) %all-to-all-start.2) | async-done | bytes 1048608 | tf_op jit(solution)/shard_map/all_to_all | solution.py:497
  433.7 57.1 %while.42 = (s32[]{:T(128)}, f32[1024,2,64]{0,2,1:T(8,128)}, f32[1024,2,64]{0,2,1:T(8,128)}, f32[2,512,2,64]{1,0,3,2:T(2,128)}, s32[2]{0:T(128)S(1)}, /*index=5*...) while((s32[]{:T(128)}, f32[1024,2,64]{0,2,1:T(8,128)}, ...), condition=%wide.region_10.11_spmd.clone, body=%wide.region_8.10_spmd.clone.sunk | while | flops 688061952 | bytes 71467456 | solution.py:349
  441.0 4.2 multiply_reduce_fusion.8
  450.6 3.7 fusion.258
  456.4 5.7 dynamic_update_slice.56
  463.4 3.7 fusion.256
  469.5 4.2 multiply_reduce_fusion.8
  479.1 3.7 fusion.258
  485.0 5.7 dynamic_update_slice.56
  496.3 19.2 %shard_map.280 = (f32[1,1024,384]{2,1,0:T(8,128)S(1)}, f32[1,1024,128]{2,1,0:T(8,128)S(1)}, f32[1,1024,128]{2,1,0:T(8,128)S(1)}, f32[1,1024,6]{2,1,0:T(8,128)S(1...) custom-call(f32[1,1024,384]{2,1,0:T(8,128)S(1)} %slice.326.x_ref, ...), custom_call_target="tpu_custom_call" | custom-call | flops 20000000000 | bytes 12000000 | tf_op jit(solution)/shard_map/pallas_call | solution.py:243
  524.7 5.7 multiply_reduce_fusion.3
  541.3 17.9 %collective-permute-done.7 = bf16[2,2,2,64,1024]{4,3,2,1,0:T(8,128)(2,1)} collective-permute-done((bf16[2,2,2,64,1024]{4,3,2,1,0:T(8,128)(2,1)}, bf16[2,2,2,64,1024]{4,3,2,1,0:T(8,128)(2,1)}, u32[]{:S(2)}, u32[]{:S(2)}) %collective-permute-start.7) | collective-permute-done | bytes 1048608 | tf_op jit(solution)/shard_map/ppermute | solution.py:362
  564.7 8.9 %collective-permute-done.8 = bf16[2,2,64,1024]{3,2,1,0:T(8,128)(2,1)S(1)} collective-permute-done((bf16[2,2,64,1024]{3,2,1,0:T(8,128)(2,1)S(1)}, bf16[2,2,64,1024]{3,2,1,0:T(8,128)(2,1)S(1)}, u32[]{:S(2)}, u32[]{:S(2)}) %collective-permute-start.8) | collective-permute-done | bytes 524320 | tf_op jit(solution)/shard_map/ppermute | solution.py:362
  580.5 6.5 collective-permute-done.9
  596.7 3.8 concatenate.146
  604.8 3.8 all-to-all-start.3
  611.3 22.9 %all-to-all-done.3 = bf16[4,1,256,1024]{2,3,1,0:T(8,128)(2,1)S(1)} async-done(((bf16[4,1,256,1024]{2,3,1,0:T(8,128)(2,1)}), bf16[4,1,256,1024]{2,3,1,0:T(8,128)(2,1)S(1)}, u32[]{:S(2)}, u32[]{:S(2)}) %all-to-all-start.3) | async-done | bytes 2097184 | tf_op jit(solution)/shard_map/all_to_all | solution.py:497
  638.6 5.2 fusion.53
  652.1 4.7 convolution_convert_fusion
  697.8 17.0 %collective-permute-done.23 = bf16[2,2,2,32,2048]{4,3,2,1,0:T(8,128)(2,1)} collective-permute-done((bf16[2,2,2,32,2048]{4,3,2,1,0:T(8,128)(2,1)}, bf16[2,2,2,32,2048]{4,3,2,1,0:T(8,128)(2,1)}, u32[]{:S(2)}, u32[]{:S(2)}) %collective-permute-start.23) | collective-permute-done | bytes 1048608 | tf_op jit(solution)/shard_map/ppermute | solution.py:362
  725.0 4.6 collective-permute-done.24
  735.2 12.5 %collective-permute-done.25 = bf16[2,32,2048]{2,1,0:T(8,128)(2,1)S(1)} collective-permute-done((bf16[2,32,2048]{2,1,0:T(8,128)(2,1)S(1)}, bf16[2,32,2048]{2,1,0:T(8,128)(2,1)S(1)}, u32[]{:S(2)}, u32[]{:S(2)}) %collective-permute-start.25) | collective-permute-done | bytes 262176 | tf_op jit(solution)/shard_map/ppermute | solution.py:362
  747.9 5.8 collective-permute-done.30
  (653 shorter events, 291.5 us)
Async XLA Ops:
  7.2 94.9 %all-gather.7.cloned.1.call-start = ((), (), s32[]{:S(2)}) async-start(), calls=%async_computation.6 | async-start | bytes 8921088 | tf_op jit(solution)/shard_map/all_gather | solution.py:460
  11.3 190.4 %all-gather.11.cloned.1.call-start = ((), (), s32[]{:S(2)}) async-start(), calls=%async_computation.8 | async-start | bytes 1179648 | tf_op jit(solution)/shard_map/all_gather | solution.py:470
  12.0 189.6 %all-gather.9.cloned.1.call-start = ((), (), s32[]{:S(2)}) async-start(), calls=%async_computation.7 | async-start | bytes 2359296 | tf_op jit(solution)/shard_map/all_gather | solution.py:469
  12.1 19.8 %collective-permute-start = (bf16[1,256,1024]{2,1,0:T(8,128)(2,1)}, bf16[1,256,1024]{2,1,0:T(8,128)(2,1)S(1)}, u32[]{:S(2)}, u32[]{:S(2)}) collective-permute-start(bf16[1,256,1024]{2,1,0:T(8,128)(2,1)} %param.21), channel_id=1, source_target_pairs={{1,0},{2,1},{3,2},{5,4},{6,5},{7,6},{9,8},{10,9},{11,10},{13,12},{... | collective-permute-start | bytes 1572872 | tf_op jit(solution)/shard_map/ppermute | solution.py:404
  13.4 22.8 %collective-permute-start.3 = (bf16[1,256,1024]{2,1,0:T(8,128)(2,1)}, bf16[1,256,1024]{2,1,0:T(8,128)(2,1)S(1)}, u32[]{:S(2)}, u32[]{:S(2)}) collective-permute-start(bf16[1,256,1024]{2,1,0:T(8,128)(2,1)} %param.21), channel_id=1, source_target_pairs={{0,1},{1,2},{2,3},{4,5},{5,6},{6,7},{8,9},{9,10},{10,11},{12,13},{... | collective-permute-start | bytes 1572872 | tf_op jit(solution)/shard_map/ppermute | solution.py:403
  31.9 22.5 %collective-permute-start.1 = (bf16[1,256,1024]{2,1,0:T(8,128)(2,1)S(1)}, bf16[1,256,1024]{2,1,0:T(8,128)(2,1)S(1)}, u32[]{:S(2)}, u32[]{:S(2)}) collective-permute-start(bf16[1,256,1024]{2,1,0:T(8,128)(2,1)S(1)} %collective-permute-done), channel_id=1, source_target_pairs={{1,0},{2,1},{3,2},{5,4},{6,5},{7,6},{9,8},{10,9},{11,10},{13,12},{... | collective-permute-start | bytes 1572872 | tf_op jit(solution)/shard_map/ppermute | solution.py:404
  36.2 24.8 %collective-permute-start.4 = (bf16[1,256,1024]{2,1,0:T(8,128)(2,1)S(1)}, bf16[1,256,1024]{2,1,0:T(8,128)(2,1)S(1)}, u32[]{:S(2)}, u32[]{:S(2)}) collective-permute-start(bf16[1,256,1024]{2,1,0:T(8,128)(2,1)S(1)} %collective-permute-done.3), channel_id=1, source_target_pairs={{0,1},{1,2},{2,3},{4,5},{5,6},{6,7},{8,9},{9,10},{10,11},{12,13},{... | collective-permute-start | bytes 1572872 | tf_op jit(solution)/shard_map/ppermute | solution.py:403
  54.3 16.0 %collective-permute-start.2 = (bf16[1,256,1024]{2,1,0:T(8,128)(2,1)S(1)}, bf16[1,256,1024]{2,1,0:T(8,128)(2,1)S(1)}, u32[]{:S(2)}, u32[]{:S(2)}) collective-permute-start(bf16[1,256,1024]{2,1,0:T(8,128)(2,1)S(1)} %collective-permute-done.1), channel_id=1, source_target_pairs={{1,0},{2,1},{3,2},{5,4},{6,5},{7,6},{9,8},{10,9},{11,10},{13,12},{... | collective-permute-start | bytes 1572872 | tf_op jit(solution)/shard_map/ppermute | solution.py:404
  61.0 14.4 %collective-permute-start.5 = (bf16[1,256,1024]{2,1,0:T(8,128)(2,1)S(1)}, bf16[1,256,1024]{2,1,0:T(8,128)(2,1)S(1)}, u32[]{:S(2)}, u32[]{:S(2)}) collective-permute-start(bf16[1,256,1024]{2,1,0:T(8,128)(2,1)S(1)} %collective-permute-done.4), channel_id=1, source_target_pairs={{0,1},{1,2},{2,3},{4,5},{5,6},{6,7},{8,9},{9,10},{10,11},{12,13},{... | collective-permute-start | bytes 1572872 | tf_op jit(solution)/shard_map/ppermute | solution.py:403
  67.4 46.1 %copy-start.112 = (f32[256]{0:T(256)}, f32[256]{0:T(256)S(1)}, u32[]{:S(2)}) copy-start(f32[256]{0:T(256)S(1)} %get-tuple-element.589) | copy-start | bytes 3076
  120.0 32.2 %all-to-all-start = ((bf16[4,1,256,1024]{3,2,1,0:T(8,128)(2,1)}), bf16[4,1,256,1024]{3,2,1,0:T(8,128)(2,1)S(1)}, u32[]{:S(2)}, u32[]{:S(2)}) async-start(bf16[4,1,256,1024]{3,2,1,0:T(8,128)(2,1)} %concatenate.127), calls=%async_computation | async-start | bytes 4194304 | tf_op jit(solution)/shard_map/all_to_all | solution.py:497
  123.8 102.8 %all-gather.15.cloned.1.call-start = ((), (), s32[]{:S(2)}) async-start(), calls=%async_computation.12 | async-start | bytes 4325376 | tf_op jit(solution)/shard_map/all_gather | solution.py:468
  156.2 35.3 %copy-start.1 = (f32[1,1024,6]{2,1,0:T(8,128)}, f32[1,1024,6]{2,1,0:T(8,128)S(1)}, u32[]{:S(2)}) copy-start(f32[1,1024,6]{2,1,0:T(8,128)S(1)} %get-tuple-element.557.step_ref) | copy-start | bytes 73732
  227.8 18.8 %all-to-all-start.1 = ((bf16[4,1,256,512]{2,3,1,0:T(8,128)(2,1)}), bf16[4,1,256,512]{2,3,1,0:T(8,128)(2,1)}, u32[]{:S(2)}, u32[]{:S(2)}) async-start(bf16[4,1,256,512]{2,3,1,0:T(8,128)(2,1)} %copy.286), calls=%async_computation.1 | async-start | bytes 2097152 | tf_op jit(solution)/shard_map/all_to_all | solution.py:497
  232.1 68.9 %all-gather.13.cloned.1.call-start = ((), (), s32[]{:S(2)}) async-start(), calls=%async_computation.9 | async-start | bytes 2621440 | tf_op jit(solution)/shard_map/all_gather | solution.py:623
  255.4 149.9 %copy-start.26 = (f32[1,256,1024]{2,1,0:T(8,128)}, f32[1,256,1024]{2,1,0:T(8,128)S(1)}, u32[]{:S(2)}) copy-start(f32[1,256,1024]{2,1,0:T(8,128)S(1)} %get-tuple-element.595) | copy-start | bytes 3145732
  255.4 149.9 %copy-start.114 = (f32[256]{0:T(256)}, f32[256]{0:T(256)S(1)}, u32[]{:S(2)}) copy-start(f32[256]{0:T(256)S(1)} %get-tuple-element.590) | copy-start | bytes 3076
  256.5 101.3 %reduce-scatter.3.cloned.1.call-start = ((), (), s32[]{:S(2)}) async-start(), calls=%async_computation.10 | async-start | bytes 2621440 | tf_op jit(solution)/shard_map/reduce_scatter | solution.py:643
  313.9 88.3 %reduce-scatter.5.cloned.1.call-start = ((), (), s32[]{:S(2)}) async-start(), calls=%async_computation.11 | async-start | bytes 2621440 | tf_op jit(solution)/shard_map/reduce_scatter | solution.py:631
  326.4 7.5 collective-permute-start.11
  328.6 2.4 collective-permute-start.14
  332.2 8.6 %collective-permute-start.15 = (bf16[2,128,512]{2,1,0:T(8,128)(2,1)S(1)}, bf16[2,128,512]{2,1,0:T(8,128)(2,1)S(1)}, u32[]{:S(2)}, u32[]{:S(2)}) collective-permute-start(bf16[2,128,512]{2,1,0:T(8,128)(2,1)S(1)} %dynamic-slice_bitcast_fusion.11), channel_id=1, source_target_pairs={{0,8},{4,12},{8,0},{12,4},{1,9},{5,13},{9,1},{13,5},{2,10},{6,14},... | collective-permute-start | bytes 786440 | tf_op jit(solution)/shard_map/ppermute | solution.py:362
  338.7 14.2 %collective-permute-start.12 = (bf16[2,128,2,512]{3,2,1,0:T(2,128)(2,1)}, bf16[2,128,2,512]{3,2,1,0:T(2,128)(2,1)}, u32[]{:S(2)}, u32[]{:S(2)}) collective-permute-start(bf16[2,128,2,512]{3,2,1,0:T(2,128)(2,1)} %dynamic-slice_bitcast_fusion.7), channel_id=1, source_target_pairs={{0,8},{4,12},{8,0},{12,4},{1,9},{5,13},{9,1},{13,5},{2,10},{6,14},... | collective-permute-start | bytes 1572872 | tf_op jit(solution)/shard_map/ppermute | solution.py:362
  342.3 7.5 collective-permute-start.16
  349.8 55.5 %copy-start.47 = (bf16[1,256,1024]{2,1,0:T(8,128)(2,1)S(1)}, bf16[1,256,1024]{2,1,0:T(8,128)(2,1)}, u32[]{:S(2)}) copy-start(bf16[1,256,1024]{2,1,0:T(8,128)(2,1)} %param.21) | copy-start | bytes 1572868
  356.4 58.9 %collective-permute-start.13 = (bf16[128,2,512]{2,1,0:T(2,128)(2,1)}, bf16[128,2,512]{2,1,0:T(2,128)(2,1)}, u32[]{:S(2)}, u32[]{:S(2)}) collective-permute-start(bf16[128,2,512]{2,1,0:T(2,128)(2,1)} %dynamic-slice_bitcast_fusion.12), channel_id=1, source_target_pairs={{0,16},{16,0},{1,17},{17,1},{2,18},{18,2},{3,19},{19,3},{4,20},{20... | collective-permute-start | bytes 786440 | tf_op jit(solution)/shard_map/ppermute | solution.py:362
  411.7 18.0 %all-to-all-start.2 = ((bf16[4,1,256,512]{3,2,1,0:T(8,128)(2,1)}), bf16[4,1,256,512]{3,2,1,0:T(8,128)(2,1)S(1)}, u32[]{:S(2)}, u32[]{:S(2)}) async-start(bf16[4,1,256,512]{3,2,1,0:T(8,128)(2,1)} %pad_maximum_fusion.8), calls=%async_computation.3 | async-start | bytes 2097152 | tf_op jit(solution)/shard_map/all_to_all | solution.py:497
  421.2 109.2 %collective-permute-start.6 = (bf16[2,2,2,2,64,1024]{5,4,3,2,1,0:T(8,128)(2,1)}, bf16[2,2,2,2,64,1024]{5,4,3,2,1,0:T(8,128)(2,1)}, u32[]{:S(2)}, u32[]{:S(2)}) collective-permute-start(bf16[2,2,2,2,64,1024]{5,4,3,2,1,0:T(8,128)(2,1)} %fusion.68), channel_id=1, source_target_pairs={{0,4},{4,0},{8,12},{12,8},{1,5},{5,1},{9,13},{13,9},{2,6},{6,2},{1... | collective-permute-start | bytes 6291464 | tf_op jit(solution)/shard_map/ppermute | solution.py:362
  534.2 25.0 %collective-permute-start.7 = (bf16[2,2,2,64,1024]{4,3,2,1,0:T(8,128)(2,1)}, bf16[2,2,2,64,1024]{4,3,2,1,0:T(8,128)(2,1)}, u32[]{:S(2)}, u32[]{:S(2)}) collective-permute-start(bf16[2,2,2,64,1024]{4,3,2,1,0:T(8,128)(2,1)} %dynamic-slice_bitcast_fusion.4), channel_id=1, source_target_pairs={{0,8},{4,12},{8,0},{12,4},{1,9},{5,13},{9,1},{13,5},{2,10},{6,14},... | collective-permute-start | bytes 3145736 | tf_op jit(solution)/shard_map/ppermute | solution.py:362
  560.9 12.6 %collective-permute-start.8 = (bf16[2,2,64,1024]{3,2,1,0:T(8,128)(2,1)S(1)}, bf16[2,2,64,1024]{3,2,1,0:T(8,128)(2,1)S(1)}, u32[]{:S(2)}, u32[]{:S(2)}) collective-permute-start(bf16[2,2,64,1024]{3,2,1,0:T(8,128)(2,1)S(1)} %dynamic-slice_bitcast_fusion.8), channel_id=1, source_target_pairs={{0,16},{16,0},{1,17},{17,1},{2,18},{18,2},{3,19},{19,3},{4,20},{20... | collective-permute-start | bytes 1572872 | tf_op jit(solution)/shard_map/ppermute | solution.py:362
  575.3 11.7 %collective-permute-start.9 = (bf16[2,64,1024]{2,1,0:T(8,128)(2,1)}, bf16[2,64,1024]{2,1,0:T(8,128)(2,1)}, u32[]{:S(2)}, u32[]{:S(2)}) collective-permute-start(bf16[2,64,1024]{2,1,0:T(8,128)(2,1)} %dynamic-slice_bitcast_fusion.13), channel_id=1, source_target_pairs={{0,2},{1,3},{2,0},{3,1},{4,6},{5,7},{6,4},{7,5},{8,10},{9,11},{10,... | collective-permute-start | bytes 786440 | tf_op jit(solution)/shard_map/ppermute | solution.py:362
  588.9 11.6 %collective-permute-start.10 = (bf16[64,1024]{1,0:T(8,128)(2,1)}, bf16[64,1024]{1,0:T(8,128)(2,1)}, u32[]{:S(2)}, u32[]{:S(2)}) collective-permute-start(bf16[64,1024]{1,0:T(8,128)(2,1)} %dynamic-slice_bitcast_fusion.17), channel_id=1, source_target_pairs={{0,1},{1,0},{2,3},{3,2},{4,5},{5,4},{6,7},{7,6},{8,9},{9,8},{10,11... | collective-permute-start | bytes 393224 | tf_op jit(solution)/shard_map/ppermute | solution.py:362
  604.8 29.4 %all-to-all-start.3 = ((bf16[4,1,256,1024]{2,3,1,0:T(8,128)(2,1)}), bf16[4,1,256,1024]{2,3,1,0:T(8,128)(2,1)S(1)}, u32[]{:S(2)}, u32[]{:S(2)}) async-start(bf16[4,1,256,1024]{2,3,1,0:T(8,128)(2,1)} %copy.315), calls=%async_computation.5 | async-start | bytes 4194304 | tf_op jit(solution)/shard_map/all_to_all | solution.py:497
  656.9 12.7 %collective-permute-start.17 = (f32[88,128]{1,0:T(8,128)S(1)}, f32[88,128]{1,0:T(8,128)S(1)}, u32[]{:S(2)}, u32[]{:S(2)}) collective-permute-start(f32[88,128]{1,0:T(8,128)S(1)} %bitcast.535), channel_id=1, source_target_pairs={{0,16},{16,0},{1,17},{17,1},{2,18},{18,2},{3,19},{19,3},{4,20},{20... | collective-permute-start | bytes 135176 | tf_op jit(solution)/shard_map/ppermute | solution.py:393
  664.8 23.0 %collective-permute-start.22 = (bf16[2,2,2,2,32,2048]{5,4,3,2,0,1:T(8,128)(2,1)}, bf16[2,2,2,2,32,2048]{5,4,3,2,0,1:T(8,128)(2,1)}, u32[]{:S(2)}, u32[]{:S(2)}) collective-permute-start(bf16[2,2,2,2,32,2048]{5,4,3,2,0,1:T(8,128)(2,1)} %bitcast.447), channel_id=1, source_target_pairs={{0,4},{4,0},{8,12},{12,8},{1,5},{5,1},{9,13},{13,9},{2,6},{6,2},{1... | collective-permute-start | bytes 6291464 | tf_op jit(solution)/shard_map/ppermute | solution.py:362
  669.6 22.4 %collective-permute-start.27 = (bf16[2,2,2,2,32,2072]{5,4,3,2,1,0:T(8,128)(2,1)}, bf16[2,2,2,2,32,2072]{5,4,3,2,1,0:T(8,128)(2,1)}, u32[]{:S(2)}, u32[]{:S(2)}) collective-permute-start(bf16[2,2,2,2,32,2072]{5,4,3,2,1,0:T(8,128)(2,1)} %dynamic-slice_bitcast_fusion.1), channel_id=1, source_target_pairs={{0,4},{4,0},{8,12},{12,8},{1,5},{5,1},{9,13},{13,9},{2,6},{6,2},{1... | collective-permute-start | bytes 6365192 | tf_op jit(solution)/shard_map/ppermute | solution.py:362
  669.7 4.0 collective-permute-start.18
  673.7 4.1 collective-permute-start.19
  677.9 4.1 collective-permute-start.20
  682.0 5.7 collective-permute-start.21
  691.6 23.2 %collective-permute-start.23 = (bf16[2,2,2,32,2048]{4,3,2,1,0:T(8,128)(2,1)}, bf16[2,2,2,32,2048]{4,3,2,1,0:T(8,128)(2,1)}, u32[]{:S(2)}, u32[]{:S(2)}) collective-permute-start(bf16[2,2,2,32,2048]{4,3,2,1,0:T(8,128)(2,1)} %dynamic-slice_bitcast_fusion.3), channel_id=1, source_target_pairs={{0,8},{4,12},{8,0},{12,4},{1,9},{5,13},{9,1},{13,5},{2,10},{6,14},... | collective-permute-start | bytes 3145736 | tf_op jit(solution)/shard_map/ppermute | solution.py:362
  694.3 26.1 %collective-permute-start.28 = (bf16[2,2,2,32,2072]{4,3,2,1,0:T(8,128)(2,1)S(1)}, bf16[2,2,2,32,2072]{4,3,2,1,0:T(8,128)(2,1)}, u32[]{:S(2)}, u32[]{:S(2)}) collective-permute-start(bf16[2,2,2,32,2072]{4,3,2,1,0:T(8,128)(2,1)S(1)} %dynamic-slice_bitcast_fusion.2), channel_id=1, source_target_pairs={{0,16},{16,0},{1,17},{17,1},{2,18},{18,2},{3,19},{19,3},{4,20},{20... | collective-permute-start | bytes 3182600 | tf_op jit(solution)/shard_map/ppermute | solution.py:362
  716.8 12.8 %collective-permute-start.24 = (bf16[2,2,32,2048]{3,2,1,0:T(8,128)(2,1)S(1)}, bf16[2,2,32,2048]{3,2,1,0:T(8,128)(2,1)S(1)}, u32[]{:S(2)}, u32[]{:S(2)}) collective-permute-start(bf16[2,2,32,2048]{3,2,1,0:T(8,128)(2,1)S(1)} %dynamic-slice_bitcast_fusion.6), channel_id=1, source_target_pairs={{0,16},{16,0},{1,17},{17,1},{2,18},{18,2},{3,19},{19,3},{4,20},{20... | collective-permute-start | bytes 1572872 | tf_op jit(solution)/shard_map/ppermute | solution.py:362
  722.0 10.6 %collective-permute-start.29 = (bf16[2,2,32,2072]{3,2,1,0:T(8,128)(2,1)S(1)}, bf16[2,2,32,2072]{3,2,1,0:T(8,128)(2,1)S(1)}, u32[]{:S(2)}, u32[]{:S(2)}) collective-permute-start(bf16[2,2,32,2072]{3,2,1,0:T(8,128)(2,1)S(1)} %dynamic-slice_bitcast_fusion.5), channel_id=1, source_target_pairs={{0,8},{4,12},{8,0},{12,4},{1,9},{5,13},{9,1},{13,5},{2,10},{6,14},... | collective-permute-start | bytes 1591304 | tf_op jit(solution)/shard_map/ppermute | solution.py:362
  729.7 18.0 %collective-permute-start.25 = (bf16[2,32,2048]{2,1,0:T(8,128)(2,1)S(1)}, bf16[2,32,2048]{2,1,0:T(8,128)(2,1)S(1)}, u32[]{:S(2)}, u32[]{:S(2)}) collective-permute-start(bf16[2,32,2048]{2,1,0:T(8,128)(2,1)S(1)} %dynamic-slice_bitcast_fusion.10), channel_id=1, source_target_pairs={{0,2},{1,3},{2,0},{3,1},{4,6},{5,7},{6,4},{7,5},{8,10},{9,11},{10,... | collective-permute-start | bytes 786440 | tf_op jit(solution)/shard_map/ppermute | solution.py:362
  732.7 21.0 %collective-permute-start.30 = (bf16[2,32,2072]{2,1,0:T(8,128)(2,1)S(1)}, bf16[2,32,2072]{2,1,0:T(8,128)(2,1)S(1)}, u32[]{:S(2)}, u32[]{:S(2)}) collective-permute-start(bf16[2,32,2072]{2,1,0:T(8,128)(2,1)S(1)} %dynamic-slice_bitcast_fusion.9), channel_id=1, source_target_pairs={{0,2},{1,3},{2,0},{3,1},{4,6},{5,7},{6,4},{7,5},{8,10},{9,11},{10,... | collective-permute-start | bytes 795656 | tf_op jit(solution)/shard_map/ppermute | solution.py:362
  747.8 8.6 %collective-permute-start.26 = (bf16[32,2048]{1,0:T(8,128)(2,1)S(1)}, bf16[32,2048]{1,0:T(8,128)(2,1)S(1)}, u32[]{:S(2)}, u32[]{:S(2)}) collective-permute-start(bf16[32,2048]{1,0:T(8,128)(2,1)S(1)} %dynamic-slice_bitcast_fusion.15), channel_id=1, source_target_pairs={{0,1},{1,0},{2,3},{3,2},{4,5},{5,4},{6,7},{7,6},{8,9},{9,8},{10,11... | collective-permute-start | bytes 393224 | tf_op jit(solution)/shard_map/ppermute | solution.py:362
  753.8 5.6 collective-permute-start.31
  (152 other events, 978.6 us)
Sparse Core Ops, SparseCore 0:
  11.5 90.5 all-gather.6
  104.0 23.8 all-gather.10
  129.7 31.1 all-gather.8
  164.4 62.0 all-gather.14
  256.7 44.2 all-gather.12
  314.0 42.5 reduce-scatter.2
  359.0 43.1 reduce-scatter.4
